TPU v7x, 32 devices: a whole 2x2x4 slice. The times are simulated.
32 devices in a mesh: ctx: 16 (over z, x, core), head: 2 (over y).
Axes of the slice: x: 2, y: 2, z: 4, core: 2. Of those that a mesh axis runs over, the one named last changes fastest.
Arguments:
- vid_query: bfloat16 [8, 4096, 128], P('head', 'ctx')
- vid_key: bfloat16 [8, 4096, 128], P('head', 'ctx')
- vid_value: bfloat16 [8, 4096, 128], P('head', 'ctx'), may hold values from -6 to 6
- vid_out: bfloat16 [8, 4096, 128], P('head', 'ctx'), may hold values from -6 to 6
- vid_grad: bfloat16 [8, 4096, 128], P('head', 'ctx'), may hold values from -96 to 96
- vid_lse: float32 [8, 4096], P('head', 'ctx'), as said below
- vid_mask: int32 [8, 4096, 128], P('head', 'ctx'), may hold values from 0 to 255
- aud_query: bfloat16 [8, 1024, 128], P('head', 'ctx')
- aud_key: bfloat16 [8, 1024, 128], P('head', 'ctx')
- aud_value: bfloat16 [8, 1024, 128], P('head', 'ctx'), may hold values from -6 to 6
- aud_out: bfloat16 [8, 1024, 128], P('head', 'ctx'), may hold values from -6 to 6
- aud_grad: bfloat16 [8, 1024, 128], P('head', 'ctx'), may hold values from -384 to 384
- aud_lse: float32 [8, 1024], P('head', 'ctx'), as said below
- aud_mask: int32 [8, 1024, 512], P('head', None, 'ctx'), may hold values from 0 to 255
- gain_vq: float32 [8, 128], P('head'), may hold values from 0.5 to 1.5
- gain_ak: float32 [8, 128], P('head'), may hold values from 0.5 to 1.5
- gain_aq: float32 [8, 128], P('head'), may hold values from 0.5 to 1.5
- gain_vk: float32 [8, 128], P('head'), may hold values from 0.5 to 1.5
Outputs:
- grad_vid_query: bfloat16 [8, 4096, 128], P('head', 'ctx')
- grad_vid_key: bfloat16 [8, 4096, 128], P('head', 'ctx')
- grad_vid_value: bfloat16 [8, 4096, 128], P('head', 'ctx')
- grad_aud_query: bfloat16 [8, 1024, 128], P('head', 'ctx')
- grad_aud_key: bfloat16 [8, 1024, 128], P('head', 'ctx')
- grad_aud_value: bfloat16 [8, 1024, 128], P('head', 'ctx')
Inputs may be any that keep to these rules, and one draw needn't show every extreme that they name: `vid_lse`: every entry lies between ln(1024) and ln(1024) + 1.5. `aud_lse`: every entry lies between ln(4096) and ln(4096) + 1.5.
All inputs are finite; a program needn't handle non-finite values.
Results may differ from a plain program's by a relative error of at most 0.011.
Values may be sent and summed in bfloat16 or wider, within the bound.
A program may use at most 128 MiB of HBM per device.

v0:
```python
import math

import jax
import jax.numpy as jnp
from jax import lax
from jax.sharding import PartitionSpec as P

EPS = 1e-06


def unpack_bits(word_rows):
    shifts = jnp.arange(8, dtype=jnp.int32)
    bit_values = jnp.bitwise_and(jnp.right_shift(word_rows[..., None], shifts), 1)
    return bit_values.reshape(word_rows.shape[:-1] + (word_rows.shape[-1] * 8,)).astype(jnp.float32)


def dot_rows(left, right):
    return lax.dot_general(
        left, right, (((2,), (2,)), ((0,), (0,))), preferred_element_type=jnp.float32
    )


def dot_cols(left, right):
    return lax.dot_general(
        left, right, (((1,), (1,)), ((0,), (0,))), preferred_element_type=jnp.float32
    )


def dot_plain(left, right):
    return lax.dot_general(
        left, right, (((2,), (1,)), ((0,), (0,))), preferred_element_type=jnp.float32
    )


def add_rows(buffer, update, offset):
    current = lax.dynamic_slice_in_dim(buffer, offset, update.shape[1], 1)
    return lax.dynamic_update_slice_in_dim(buffer, current + update, offset, 1)


def square_sums(tokens):
    values = tokens.astype(jnp.float32)
    return jnp.sum(values * values, axis=(0, 2))


def normalize(tokens, scales, gain_rows):
    return (tokens.astype(jnp.float32) * scales[None, :, None] * gain_rows[:, None, :]).astype(
        jnp.bfloat16
    )


def norm_parts(tokens, scales, gain_rows, upstream):
    weighted = upstream * gain_rows[:, None, :]
    unit_rows = tokens.astype(jnp.float32) * scales[None, :, None]
    return (weighted, unit_rows, jnp.sum(weighted * unit_rows, axis=(0, 2)))


def norm_finish(weighted, unit_rows, scales, product, feature_count):
    mean_term = product / feature_count
    return (scales[None, :, None] * (weighted - unit_rows * mean_term[None, :, None])).astype(
        jnp.bfloat16
    )


def block_terms(
    query_rows, key_rows, value_rows, upstream, lse_rows, delta_rows, word_rows, score_scale
):
    scores = dot_rows(query_rows, key_rows) * score_scale
    attention = jnp.exp(scores - lse_rows[:, :, None])
    kept_mask = unpack_bits(word_rows)
    dropped = (2.0 * kept_mask * attention).astype(jnp.bfloat16)
    prob_grad = 2.0 * kept_mask * dot_rows(upstream, value_rows)
    score_grad = (attention * (prob_grad - delta_rows[:, :, None])).astype(jnp.bfloat16)
    return (dropped, score_grad)


def local(
    vid_query,
    vid_key,
    vid_value,
    vid_out,
    vid_grad,
    vid_lse,
    vid_mask,
    aud_query,
    aud_key,
    aud_value,
    aud_out,
    aud_grad,
    aud_lse,
    aud_mask,
    gain_vq,
    gain_ak,
    gain_aq,
    gain_vk,
):
    head_count = vid_query.shape[0]
    head_dim = vid_query.shape[2]
    feature_count = lax.axis_size("head") * head_count * head_dim
    score_scale = head_dim ** (-0.5)
    total_vq, total_ak, total_aq, total_vk = lax.psum(
        (
            square_sums(vid_query),
            square_sums(aud_key),
            square_sums(aud_query),
            square_sums(vid_key),
        ),
        "head",
    )
    scale_vq = lax.rsqrt(total_vq / feature_count + EPS)
    scale_ak = lax.rsqrt(total_ak / feature_count + EPS)
    scale_aq = lax.rsqrt(total_aq / feature_count + EPS)
    scale_vk = lax.rsqrt(total_vk / feature_count + EPS)
    normed_vq = normalize(vid_query, scale_vq, gain_vq)
    normed_ak = normalize(aud_key, scale_ak, gain_ak)
    normed_aq = normalize(aud_query, scale_aq, gain_aq)
    normed_vk = normalize(vid_key, scale_vk, gain_vk)
    video_delta = jnp.sum(vid_grad.astype(jnp.float32) * vid_out.astype(jnp.float32), axis=2)
    audio_delta = jnp.sum(aud_grad.astype(jnp.float32) * aud_out.astype(jnp.float32), axis=2)
    lse_whole, delta_whole = (
        lax.all_gather(aud_lse, "ctx", axis=1, tiled=True),
        lax.all_gather(audio_delta, "ctx", axis=1, tiled=True),
    )
    audio_total = lse_whole.shape[1]
    local_video = vid_value.shape[1]

    def video_side(key_rows, value_rows, offset):
        word_rows = lax.dynamic_slice_in_dim(vid_mask, offset // 8, key_rows.shape[1] // 8, 2)
        return block_terms(
            normed_vq, key_rows, value_rows, vid_grad, vid_lse, video_delta, word_rows, score_scale
        )

    starting = (
        jnp.zeros((head_count, local_video, head_dim), jnp.float32),
        jnp.zeros((head_count, audio_total, head_dim), jnp.float32),
        jnp.zeros((head_count, audio_total, head_dim), jnp.float32),
    )
    key_piece = lax.all_gather(normed_ak, "ctx", axis=1, tiled=True)
    value_piece = lax.all_gather(aud_value, "ctx", axis=1, tiled=True)
    piece_block = math.gcd(key_piece.shape[1], 512)

    def key_pass(block_index, totals):
        query_total, key_total, value_total = totals
        leading = block_index * piece_block
        key_rows = lax.dynamic_slice_in_dim(key_piece, leading, piece_block, 1)
        value_rows = lax.dynamic_slice_in_dim(value_piece, leading, piece_block, 1)
        dropped, score_grad = video_side(key_rows, value_rows, leading)
        query_total = query_total + score_scale * dot_plain(score_grad, key_rows)
        key_total = add_rows(key_total, score_scale * dot_cols(score_grad, normed_vq), leading)
        value_total = add_rows(value_total, dot_cols(dropped, vid_grad), leading)
        return (query_total, key_total, value_total)

    up_vq, key_partial, value_partial = lax.fori_loop(
        0, key_piece.shape[1] // piece_block, key_pass, starting
    )
    up_ak, audio_value_grad = (
        lax.psum_scatter(key_partial, "ctx", scatter_dimension=1, tiled=True),
        lax.psum_scatter(value_partial, "ctx", scatter_dimension=1, tiled=True),
    )
    starting_video = (
        jnp.zeros((head_count, local_video, head_dim), jnp.float32),
        jnp.zeros((head_count, local_video, head_dim), jnp.float32),
        jnp.zeros((head_count, audio_total, head_dim), jnp.float32),
    )
    query_piece = lax.all_gather(normed_aq, "ctx", axis=1, tiled=True)
    grad_piece = lax.all_gather(aud_grad, "ctx", axis=1, tiled=True)
    query_piece_block = math.gcd(query_piece.shape[1], 512)

    def query_pass(block_index, totals):
        key_total, value_total, query_total = totals
        leading = block_index * query_piece_block
        query_rows = lax.dynamic_slice_in_dim(query_piece, leading, query_piece_block, 1)
        grad_rows = lax.dynamic_slice_in_dim(grad_piece, leading, query_piece_block, 1)
        lse_rows = lax.dynamic_slice_in_dim(lse_whole, leading, query_piece_block, 1)
        delta_rows = lax.dynamic_slice_in_dim(delta_whole, leading, query_piece_block, 1)
        word_rows = lax.dynamic_slice_in_dim(aud_mask, leading, query_piece_block, 1)
        dropped, score_grad = block_terms(
            query_rows,
            normed_vk,
            vid_value,
            grad_rows,
            lse_rows,
            delta_rows,
            word_rows,
            score_scale,
        )
        value_total = value_total + dot_cols(dropped, grad_rows)
        key_total = key_total + score_scale * dot_cols(score_grad, query_rows)
        query_total = add_rows(query_total, score_scale * dot_plain(score_grad, normed_vk), leading)
        return (key_total, value_total, query_total)

    up_vk, video_value_grad, query_partial = lax.fori_loop(
        0, query_piece.shape[1] // query_piece_block, query_pass, starting_video
    )
    up_aq = lax.psum_scatter(query_partial, "ctx", scatter_dimension=1, tiled=True)
    weighted_vq, unit_vq, local_vq = norm_parts(vid_query, scale_vq, gain_vq, up_vq)
    weighted_ak, unit_ak, local_ak = norm_parts(aud_key, scale_ak, gain_ak, up_ak)
    weighted_aq, unit_aq, local_aq = norm_parts(aud_query, scale_aq, gain_aq, up_aq)
    weighted_vk, unit_vk, local_vk = norm_parts(vid_key, scale_vk, gain_vk, up_vk)
    product_vq, product_ak, product_aq, product_vk = lax.psum(
        (local_vq, local_ak, local_aq, local_vk), "head"
    )
    grad_vid_query = norm_finish(weighted_vq, unit_vq, scale_vq, product_vq, feature_count)
    grad_aud_key = norm_finish(weighted_ak, unit_ak, scale_ak, product_ak, feature_count)
    grad_aud_query = norm_finish(weighted_aq, unit_aq, scale_aq, product_aq, feature_count)
    grad_vid_key = norm_finish(weighted_vk, unit_vk, scale_vk, product_vk, feature_count)
    return (
        grad_vid_query,
        grad_vid_key,
        video_value_grad.astype(jnp.bfloat16),
        grad_aud_query,
        grad_aud_key,
        audio_value_grad.astype(jnp.bfloat16),
    )


def solution(mesh):
    return jax.shard_map(
        local,
        mesh=mesh,
        in_specs=(
            P("head", "ctx", None),
            P("head", "ctx", None),
            P("head", "ctx", None),
            P("head", "ctx", None),
            P("head", "ctx", None),
            P("head", "ctx"),
            P("head", "ctx", None),
            P("head", "ctx", None),
            P("head", "ctx", None),
            P("head", "ctx", None),
            P("head", "ctx", None),
            P("head", "ctx", None),
            P("head", "ctx"),
            P("head", None, "ctx"),
            P("head", None),
            P("head", None),
            P("head", None),
            P("head", None),
        ),
        out_specs=(
            P("head", "ctx", None),
            P("head", "ctx", None),
            P("head", "ctx", None),
            P("head", "ctx", None),
            P("head", "ctx", None),
            P("head", "ctx", None),
        ),
        check_vma=False,
    )
```

profile of v0, /device:TPU:0, one launch (start us, length us, event | category | flops | bytes accessed | tf_op | source)
XLA Modules:
  0.0 376.2 jit_solution(13031474712623555317)
XLA Ops:
  9.6 5.9 %all-reduce.1 = (f32[64]{0:T(128)S(1)}, f32[256]{0:T(256)S(1)}, f32[64]{0:T(128)S(1)}, f32[256]{0:T(256)S(1)}) all-reduce(f32[64]{0:T(128)S(1)} %get-tuple-element.648, f32[256]{0:T(256)S(1)} %get-tuple-element.646, f32[64]{0:T(128)S(1)} %get-tuple-element.649, f32[256]{0:T(256)S(1)} %get-tuple-element.647), channel_id=1, replica_groups=mesh['ctx'=16,'head'=2] {'head'}, use_global_device_ids=true, to_apply=%region_3.0 | all-reduce | flops 640 | bytes 5120 | tf_op jit(solution)/shard_map/psum | solution.py:100
  21.6 22.3 %all-gather.1 = f32[16,64,4]{1,2,0:T(4,128)S(1)} all-gather(f32[1,64,4]{1,2,0:T(4,128)S(1)} %bitcast.88), channel_id=1, replica_groups=mesh['ctx'=16,'head'=2] {'ctx'}, dimensions={0}, use_global_device_ids=true | all-gather | bytes 17408 | tf_op jit(solution)/shard_map/all_gather | solution.py:121
  44.0 17.5 %all-gather = f32[16,64,4]{1,2,0:T(4,128)S(1)} all-gather(f32[1,64,4]{1,2,0:T(4,128)S(1)} %bitcast.89), channel_id=1, replica_groups=mesh['ctx'=16,'head'=2] {'ctx'}, dimensions={0}, use_global_device_ids=true | all-gather | bytes 17408 | tf_op jit(solution)/shard_map/all_gather | solution.py:120
  62.9 33.2 %all-gather.9.cloned.1.call-done = bf16[4,1024,128]{2,1,0:T(8,128)(2,1)} async-done(((bf16[4,64,128]{2,1,0:T(8,128)(2,1)}), bf16[4,1024,128]{2,1,0:T(8,128)(2,1)}) %all-gather.9.cloned.1.call-update) | async-done | bytes 1048592 | tf_op jit(solution)/shard_map/all_gather | solution.py:138
  99.0 26.4 %while.38 = (s32[]{:T(128)}, f32[4,256,128]{2,1,0:T(8,128)}, f32[4,1024,128]{2,1,0:T(8,128)}, f32[4,1024,128]{2,1,0:T(8,128)}, bf16[4,1024,128]{2,1,0:T(8,128)(2...) while((s32[]{:T(128)}, f32[4,256,128]{2,1,0:T(8,128)}, ...), condition=%wide.region_6.0_spmd.clone, body=%wide.region_5.0_spmd.clone.sunk | while | flops 681705472 | bytes 24664612 | solution.py:152
  101.6 2.1 fusion.132
  103.7 2.8 fusion.134
  106.5 3.2 fusion.135
  109.7 2.4 fusion.133
  114.7 2.1 fusion.132
  116.8 2.8 fusion.134
  119.6 3.2 fusion.135
  122.8 2.6 fusion.133
  125.5 10.3 %all-gather.11.cloned.1.call-done = bf16[4,1024,128]{2,1,0:T(8,128)(2,1)} async-done(((bf16[4,64,128]{2,1,0:T(8,128)(2,1)}), bf16[4,1024,128]{2,1,0:T(8,128)(2,1)}) %all-gather.11.cloned.1.call-update) | async-done | bytes 1048592 | tf_op jit(solution)/shard_map/all_gather | solution.py:164
  135.8 39.0 %all-gather.13.cloned.1.call-done = bf16[4,1024,128]{2,1,0:T(8,128)(2,1)} async-done(((bf16[4,64,128]{2,1,0:T(8,128)(2,1)}), bf16[4,1024,128]{2,1,0:T(8,128)(2,1)}) %all-gather.13.cloned.1.call-update) | async-done | bytes 1048592 | tf_op jit(solution)/shard_map/all_gather | solution.py:165
  176.2 36.8 %while.39 = (s32[]{:T(128)}, f32[4,256,128]{2,1,0:T(8,128)}, f32[4,256,128]{2,1,0:T(8,128)}, f32[4,1024,128]{2,1,0:T(8,128)}, bf16[4,1024,128]{2,1,0:T(8,128)(2,...) while((s32[]{:T(128)}, f32[4,256,128]{2,1,0:T(8,128)}, ...), condition=%wide.region_15.16_spmd.clone, body=%wide.region_14.15_spmd.clone.sunk | while | flops 681705472 | bytes 36238588 | solution.py:191
  180.3 2.9 copy.52
  183.4 2.9 multiply_convert_fusion.6
  186.3 2.7 fusion.147
  188.9 2.5 fusion.146
  191.5 3.0 convolution_add_fusion.3
  198.6 2.9 copy.52
  201.6 2.8 multiply_convert_fusion.6
  204.4 2.8 fusion.147
  207.2 2.7 fusion.146
  209.9 3.1 convolution_add_fusion.3
  213.8 1.8 convert_element_type.127
  216.1 22.8 %reduce-scatter.6.cloned.1.call-done = f32[4,64,128]{2,1,0:T(8,128)} async-done(((f32[4,1024,128]{2,1,0:T(8,128)}), f32[4,64,128]{2,1,0:T(8,128)}) %reduce-scatter.6.cloned.1.call-update) | async-done | bytes 131088 | tf_op jit(solution)/shard_map/reduce_scatter | solution.py:156
  240.0 63.5 %reduce-scatter.4.cloned.1.call-done = f32[4,64,128]{2,1,0:T(8,128)} async-done(((f32[4,1024,128]{2,1,0:T(8,128)}), f32[4,64,128]{2,1,0:T(8,128)}) %reduce-scatter.4.cloned.1.call-update) | async-done | bytes 131088 | tf_op jit(solution)/shard_map/reduce_scatter | solution.py:194
  304.6 4.9 %all-reduce = (f32[256]{0:T(256)S(1)}, f32[256]{0:T(256)S(1)}, f32[64]{0:T(128)S(1)}, f32[64]{0:T(128)S(1)}) all-reduce(f32[256]{0:T(256)S(1)} %fusion.54, f32[256]{0:T(256)S(1)} %fusion.60, f32[64]{0:T(128)S(1)} %fusion.78, f32[64]{0:T(128)S(1)} %fusion.72), channel_id=1, replica_groups=mesh['ctx'=16,'head'=2] {'head'}, use_global_device_ids=true, to_apply=%region_8.0 | all-reduce | flops 640 | bytes 5120 | tf_op jit(solution)/shard_map/psum | solution.py:199
  311.2 1.6 fusion.81
  314.6 53.2 %reduce-scatter.8.cloned.1.call-done = f32[4,64,128]{2,1,0:T(8,128)} async-done(((f32[4,1024,128]{2,1,0:T(8,128)}), f32[4,64,128]{2,1,0:T(8,128)}) %reduce-scatter.8.cloned.1.call-update) | async-done | bytes 131088 | tf_op jit(solution)/shard_map/reduce_scatter | solution.py:157
  (126 shorter events, 36.0 us)
Async XLA Ops:
  7.2 54.5 %copy-start.8 = (bf16[4,256,128]{2,1,0:T(8,128)(2,1)S(1)}, bf16[4,256,128]{2,1,0:T(8,128)(2,1)}, u32[]{:S(2)}) copy-start(bf16[4,256,128]{2,1,0:T(8,128)(2,1)} %param.22) | copy-start | bytes 786436
  7.2 55.5 %copy-start.6 = (bf16[4,256,128]{2,1,0:T(8,128)(2,1)S(1)}, bf16[4,256,128]{2,1,0:T(8,128)(2,1)}, u32[]{:S(2)}) copy-start(bf16[4,256,128]{2,1,0:T(8,128)(2,1)} %param.23) | copy-start | bytes 786436
  7.2 14.2 %copy-start.15 = (bf16[4,64,128]{2,1,0:T(8,128)(2,1)S(1)}, bf16[4,64,128]{2,1,0:T(8,128)(2,1)}, u32[]{:S(2)}) copy-start(bf16[4,64,128]{2,1,0:T(8,128)(2,1)} %param.33) | copy-start | bytes 196612
  7.2 14.2 %copy-start.16 = (bf16[4,64,128]{2,1,0:T(8,128)(2,1)S(1)}, bf16[4,64,128]{2,1,0:T(8,128)(2,1)}, u32[]{:S(2)}) copy-start(bf16[4,64,128]{2,1,0:T(8,128)(2,1)} %param.32) | copy-start | bytes 196612
  7.2 36.8 %copy-start.21 = (f32[4,64]{1,0:T(4,128)S(1)}, f32[4,64]{1,0:T(4,128)}, u32[]{:S(2)}) copy-start(f32[4,64]{1,0:T(4,128)} %param.34) | copy-start | bytes 3076
  7.2 54.4 %copy-start.20 = (f32[4,128]{1,0:T(4,128)S(1)}, f32[4,128]{1,0:T(4,128)}, u32[]{:S(2)}) copy-start(f32[4,128]{1,0:T(4,128)} %param.36) | copy-start | bytes 6148
  7.2 55.2 %copy-start.12 = (bf16[4,256,128]{2,1,0:T(8,128)(2,1)S(1)}, bf16[4,256,128]{2,1,0:T(8,128)(2,1)}, u32[]{:S(2)}) copy-start(bf16[4,256,128]{2,1,0:T(8,128)(2,1)} %param.25) | copy-start | bytes 786436
  7.2 55.2 %copy-start.13 = (bf16[4,256,128]{2,1,0:T(8,128)(2,1)S(1)}, bf16[4,256,128]{2,1,0:T(8,128)(2,1)}, u32[]{:S(2)}) copy-start(bf16[4,256,128]{2,1,0:T(8,128)(2,1)} %param.26) | copy-start | bytes 786436
  7.3 55.4 %copy-start.19 = (f32[4,128]{1,0:T(4,128)S(1)}, f32[4,128]{1,0:T(4,128)}, u32[]{:S(2)}) copy-start(f32[4,128]{1,0:T(4,128)} %param.39) | copy-start | bytes 6148
  7.3 55.6 %all-gather.7.cloned.1.call-start = ((), (), s32[]{:S(2)}) async-start(), calls=%async_computation.3 | async-start | bytes 1114112 | tf_op jit(solution)/shard_map/all_gather | solution.py:137
  17.1 79.0 %all-gather.9.cloned.1.call-start = ((), (), s32[]{:S(2)}) async-start(), calls=%async_computation.4 | async-start | bytes 1114112 | tf_op jit(solution)/shard_map/all_gather | solution.py:138
  17.9 117.9 %all-gather.11.cloned.1.call-start = ((), (), s32[]{:S(2)}) async-start(), calls=%async_computation.5 | async-start | bytes 1114112 | tf_op jit(solution)/shard_map/all_gather | solution.py:164
  19.5 155.3 %all-gather.13.cloned.1.call-start = ((), (), s32[]{:S(2)}) async-start(), calls=%async_computation.6 | async-start | bytes 1114112 | tf_op jit(solution)/shard_map/all_gather | solution.py:165
  20.1 218.8 %reduce-scatter.6.cloned.1.call-start = ((), (), s32[]{:S(2)}) async-start(), calls=%async_computation.8 | async-start | bytes 2228224 | tf_op jit(solution)/shard_map/reduce_scatter | solution.py:156
  62.9 36.2 %copy-start.22 = (f32[4,256]{1,0:T(4,128)S(1)}, f32[4,256]{1,0:T(4,128)}, u32[]{:S(2)}) copy-start(f32[4,256]{1,0:T(4,128)} %param.27) | copy-start | bytes 12292
  103.7 2.8 copy-start.3
  109.7 2.4 copy-start.14
  116.8 2.8 copy-start.3
  122.8 2.6 copy-start.5
  122.8 2.6 copy-start.14
  125.5 178.0 %reduce-scatter.4.cloned.1.call-start = ((), (), s32[]{:S(2)}) async-start(), calls=%async_computation.7 | async-start | bytes 2228224 | tf_op jit(solution)/shard_map/reduce_scatter | solution.py:194
  188.9 2.5 copy-start
  207.2 2.7 copy-start
  213.0 2.6 copy-start.2
  213.0 2.6 copy-start.9
  213.0 2.8 copy-start.1
  213.1 2.8 copy-start.7
  213.1 154.8 %reduce-scatter.8.cloned.1.call-start = ((), (), s32[]{:S(2)}) async-start(), calls=%async_computation.9 | async-start | bytes 2228224 | tf_op jit(solution)/shard_map/reduce_scatter | solution.py:157
  213.1 25.7 %copy-start.10 = (bf16[4,64,128]{2,1,0:T(8,128)(2,1)S(1)}, bf16[4,64,128]{2,1,0:T(8,128)(2,1)}, u32[]{:S(2)}) copy-start(bf16[4,64,128]{2,1,0:T(8,128)(2,1)} %param.30) | copy-start | bytes 196612
  213.1 25.7 %copy-start.17 = (f32[4,128]{1,0:T(4,128)S(1)}, f32[4,128]{1,0:T(4,128)}, u32[]{:S(2)}) copy-start(f32[4,128]{1,0:T(4,128)} %param.37) | copy-start | bytes 6148
  213.1 90.4 %copy-start.11 = (bf16[4,64,128]{2,1,0:T(8,128)(2,1)S(1)}, bf16[4,64,128]{2,1,0:T(8,128)(2,1)}, u32[]{:S(2)}) copy-start(bf16[4,64,128]{2,1,0:T(8,128)(2,1)} %param.29) | copy-start | bytes 196612
  213.2 90.4 %copy-start.18 = (f32[4,128]{1,0:T(4,128)S(1)}, f32[4,128]{1,0:T(4,128)}, u32[]{:S(2)}) copy-start(f32[4,128]{1,0:T(4,128)} %param.38) | copy-start | bytes 6148
  (3 other events, 4.3 us)
Sparse Core Ops, SparseCore 0:
  17.2 39.7 all-gather.6
  59.2 36.8 all-gather.8
  98.9 36.8 all-gather.10
  137.9 36.8 all-gather.12
  178.3 60.4 reduce-scatter.5
  242.9 60.5 reduce-scatter.3
  307.2 60.5 reduce-scatter.7
where the time goes:
time: 377 us; the launch traced here: 376 us
  waiting for transfers between devices  224 us (59%)
  blocking collectives  50.7 us (13%)
  matrix products  49.7 us (13%)
  local copies, waits for them, and re-layouts  19.2 us (5%)
  other arithmetic  17.8 us (5%)
  between operations  14.4 us (4%)
    reduce_scatter x1, waiting for transfers between devices, local(): lax.psum_scatter(query_partial, 'ctx', scatter_dimension=1, tiled=True)  63.5 us
    reduce_scatter x1, waiting for transfers between devices, local(): lax.psum_scatter(value_partial, 'ctx', scatter_dimension=1, tiled=True)  53.2 us
    all_gather x1, waiting for transfers between devices, local(): grad_piece = lax.all_gather(aud_grad, 'ctx', axis=1, tiled=True)  39 us
    all_gather x1, waiting for transfers between devices, local(): value_piece = lax.all_gather(aud_value, 'ctx', axis=1, tiled=True)  33.2 us
    dot_general x8, matrix products, dot_cols(): lax.dot_general(left, right, (((1,), (1,)), ((0,), (0,))), preferred_elem...  23.3 us
    reduce_scatter x1, waiting for transfers between devices, local(): lax.psum_scatter(key_partial, 'ctx', scatter_dimension=1, tiled=True)  22.8 us
    all_gather x1, blocking collectives, local(): lax.all_gather(audio_delta, 'ctx', axis=1, tiled=True)  22.3 us
    all_gather x1, blocking collectives, local(): lax.all_gather(aud_lse, 'ctx', axis=1, tiled=True)  17.5 us
  transfers between devices with their start and end apart: 7, of which 6 were waited for; matrix products, arithmetic and copies ran while one was open for 22% of the time, Pallas kernels for 0%

commit v1 on v0

v1 whole, which is shorter than its diff:
```python
import functools

import jax
import jax.numpy as jnp
from jax import lax
from jax.experimental import pallas as pl
from jax.experimental.pallas import tpu as pltpu
from jax.sharding import PartitionSpec as P

EPS = 1e-06
XS = 2
CORES = 2
CHUNK = 256
MESH = pl.DeviceIdType.MESH


def place():
    me = lax.axis_index("ctx")
    return me // (XS * CORES), lax.rem(me // CORES, XS), lax.rem(me, CORES)


def peer(z, x, c):
    return {"ctx": (z * XS + x) * CORES + c}


def enter(z, x, c, zs):
    barrier = pltpu.get_barrier_semaphore()
    targets = [peer(z, x, 1 - c), peer(z, 1 - x, c)]
    targets += [peer(lax.rem(z + d, zs), x, c) for d in range(1, zs)]
    for target in targets:
        pl.semaphore_signal(barrier, inc=1, device_id=target, device_id_type=MESH)
    pl.semaphore_wait(barrier, len(targets))


def gather_kernel(zs, big_ref, small_ref, big_out, small_out, z_send, z_recv, x_send, x_recv, c_send, c_recv, own_sem):
    z, x, c = place()
    enter(z, x, c, zs)
    pairs = ((big_ref, big_out), (small_ref, small_out))

    def slot(ref, k, zz, xx, cc):
        return ref.at[:, zz, xx, cc] if k == 0 else ref.at[zz, xx, cc]

    pending = []

    def z_copy(k, d):
        src, out = pairs[k]
        return pltpu.make_async_remote_copy(
            src_ref=src, dst_ref=slot(out, k, z, x, c), send_sem=z_send.at[k, d], recv_sem=z_recv.at[k, d],
            device_id=peer(lax.rem(z + d, zs), x, c), device_id_type=MESH)

    def x_copy(k, d):
        src, out = pairs[k]
        zz = lax.rem(z + zs - d, zs)
        there = slot(out, k, zz, x, c)
        return pltpu.make_async_remote_copy(
            src_ref=src if d == 0 else there, dst_ref=there, send_sem=x_send.at[k, d], recv_sem=x_recv.at[k, d],
            device_id=peer(z, 1 - x, c), device_id_type=MESH)

    def c_copy(k, d, side):
        src, out = pairs[k]
        zz = lax.rem(z + zs - d, zs)
        there = slot(out, k, zz, x if side == 0 else 1 - x, c)
        return pltpu.make_async_remote_copy(
            src_ref=src if d == 0 and side == 0 else there, dst_ref=there, send_sem=c_send.at[k, d, side],
            recv_sem=c_recv.at[k, d, side], device_id=peer(z, x, 1 - c), device_id_type=MESH)

    z_copies = [[z_copy(k, d) for k in range(2)] for d in range(1, zs)]
    x_copies = [[x_copy(k, d) for k in range(2)] for d in range(zs)]
    c_copies = [[[c_copy(k, d, side) for k in range(2)] for d in range(zs)] for side in range(2)]
    own = [pltpu.make_async_copy(pairs[k][0], slot(pairs[k][1], k, z, x, c), own_sem.at[k]) for k in range(2)]

    def start(group):
        for copy in group:
            copy.start()

    def arrive(group):
        for copy in group:
            copy.wait_recv()

    for group in z_copies:
        start(group)
    start(x_copies[0])
    start(c_copies[0][0])
    start(own)
    for d in range(1, zs):
        arrive(z_copies[d - 1])
        start(x_copies[d])
        start(c_copies[0][d])
    for d in range(zs):
        arrive(x_copies[d])
        start(c_copies[1][d])
    for side in range(2):
        for d in range(zs):
            arrive(c_copies[side][d])
    for copy in own:
        copy.wait()
    for group in z_copies + x_copies + c_copies[0] + c_copies[1]:
        for copy in group:
            copy.wait_send()


def gather(big, small, zs):
    rows, tokens, width = big.shape
    sems = lambda *shape: pltpu.SemaphoreType.DMA(shape)
    return pl.pallas_call(
        functools.partial(gather_kernel, zs),
        out_shape=(
            jax.ShapeDtypeStruct((rows, zs, XS, CORES, tokens, width), big.dtype),
            jax.ShapeDtypeStruct((zs, XS, CORES) + small.shape, small.dtype),
        ),
        in_specs=[pl.BlockSpec(memory_space=pltpu.VMEM)] * 2,
        out_specs=[pl.BlockSpec(memory_space=pltpu.VMEM)] * 2,
        scratch_shapes=[sems(2, zs), sems(2, zs), sems(2, zs), sems(2, zs), sems(2, zs, 2), sems(2, zs, 2), sems(2)],
        compiler_params=pltpu.CompilerParams(collective_id=0, has_side_effects=True, vmem_limit_bytes=48 << 20),
        name="gather_audio",
    )(big, small)


def scatter_kernel(zs, part_ref, out_ref, core_in, x_out, x_in, z_out, z_in, c_send, c_recv, x_send, x_recv, z_send, z_recv):
    z, x, c = place()
    enter(z, x, c, zs)
    order = list(range(1, zs)) + [0]
    target = [lax.rem(z + d, zs) for d in range(zs)]
    c_copies = [pltpu.make_async_remote_copy(
        src_ref=part_ref.at[:, target[d], :, 1 - c], dst_ref=core_in.at[d], send_sem=c_send.at[d], recv_sem=c_recv.at[d],
        device_id=peer(z, x, 1 - c), device_id_type=MESH) for d in range(zs)]
    x_copies = [pltpu.make_async_remote_copy(
        src_ref=x_out.at[d], dst_ref=x_in.at[d], send_sem=x_send.at[d], recv_sem=x_recv.at[d],
        device_id=peer(z, 1 - x, c), device_id_type=MESH) for d in range(zs)]
    z_copies = [pltpu.make_async_remote_copy(
        src_ref=z_out.at[d], dst_ref=z_in.at[d], send_sem=z_send.at[d], recv_sem=z_recv.at[d],
        device_id=peer(target[d], x, c), device_id_type=MESH) if d else None for d in range(zs)]
    for d in order:
        c_copies[d].start()

    def core_sum(d, side):
        return part_ref[:, target[d], side, c].astype(jnp.float32) + core_in[d, :, side].astype(jnp.float32)

    for d in order:
        c_copies[d].wait_recv()
        x_out[d] = core_sum(d, 1 - x).astype(x_out.dtype)
        x_copies[d].start()
    for d in order:
        x_copies[d].wait_recv()
        both = core_sum(d, x) + x_in[d].astype(jnp.float32)
        if d:
            z_out[d] = both.astype(z_out.dtype)
            z_copies[d].start()
        else:
            out_ref[...] = both
    for d in range(1, zs):
        z_copies[d].wait_recv()
        out_ref[...] += z_in[d].astype(jnp.float32)
    for d in range(zs):
        c_copies[d].wait_send()
        x_copies[d].wait_send()
        if d:
            z_copies[d].wait_send()


def scatter(part, zs):
    rows, _, _, _, tokens, width = part.shape
    sems = lambda: pltpu.SemaphoreType.DMA((zs,))
    block = lambda *lead: pltpu.VMEM(lead + (tokens, width), part.dtype)
    return pl.pallas_call(
        functools.partial(scatter_kernel, zs),
        out_shape=jax.ShapeDtypeStruct((rows, tokens, width), jnp.float32),
        in_specs=[pl.BlockSpec(memory_space=pltpu.VMEM)],
        out_specs=pl.BlockSpec(memory_space=pltpu.VMEM),
        scratch_shapes=[block(zs, rows, XS), block(zs, rows), block(zs, rows), block(zs, rows), block(zs, rows)]
        + [sems() for _ in range(6)],
        compiler_params=pltpu.CompilerParams(collective_id=1, has_side_effects=True, vmem_limit_bytes=56 << 20),
        name="scatter_audio",
    )(part)


def rows_dot(left, right):
    return lax.dot_general(left, right, (((1,), (1,)), ((), ())), preferred_element_type=jnp.float32)


def cols_dot(left, right):
    return lax.dot_general(left, right, (((0,), (0,)), ((), ())), preferred_element_type=jnp.float32)


def plain_dot(left, right):
    return lax.dot_general(left, right, (((1,), (0,)), ((), ())), preferred_element_type=jnp.float32)


def tile_terms(keys, values, queries, grads, lse, delta, words, first_key):
    nk, nw = keys.shape[0], words.shape[1]
    scale = keys.shape[1] ** (-0.5)
    key_of = lax.broadcasted_iota(jnp.int32, (nk, nw), 0) + first_key
    word_of = lax.broadcasted_iota(jnp.int32, (nk, nw), 1)
    spread = jnp.where(key_of // 8 == word_of, 1.0, 0.0).astype(jnp.bfloat16)
    spread_words = rows_dot(spread, words).astype(jnp.int32)
    shape = spread_words.shape
    bit = jnp.left_shift(1, lax.rem(lax.broadcasted_iota(jnp.int32, shape, 0), 8))
    keep = jnp.bitwise_and(spread_words, bit) != 0
    probs = jnp.exp(rows_dot(keys, queries) * scale - lse)
    dropped = jnp.where(keep, 2.0 * probs, 0.0).astype(jnp.bfloat16)
    prob_grad = jnp.where(keep, 2.0 * rows_dot(values, grads), 0.0)
    score_grad = (probs * (prob_grad - delta)).astype(jnp.bfloat16)
    return (
        plain_dot(dropped, grads),
        scale * plain_dot(score_grad, queries),
        scale * cols_dot(score_grad, keys),
    )


def attention_kernel(aud_ref, vq_ref, vk_ref, vv_ref, vg_ref, vl_ref, vd_ref, vw_ref, al_ref, ad_ref, aw_ref,
                     dvq_ref, dvk_ref, dvv_ref, part_ref):
    audio = aud_ref.shape[2]
    chunk = min(CHUNK, audio)
    vq, vk, vv, vg = vq_ref[0], vk_ref[0], vv_ref[0], vg_ref[0]
    vid_words = vw_ref[0].astype(jnp.float32).astype(jnp.bfloat16)
    for first in range(0, audio, chunk):
        rows = pl.ds(first, chunk)
        ak, av, aq, ag = (aud_ref[i, 0, rows, :] for i in range(4))
        value_grad, key_grad, query_grad = tile_terms(
            ak, av, vq, vg, vl_ref[0], vd_ref[0], vid_words, first)
        part_ref[0, 0, rows, :] = key_grad.astype(jnp.bfloat16)
        part_ref[1, 0, rows, :] = value_grad.astype(jnp.bfloat16)
        if first:
            dvq_ref[0] += query_grad
        else:
            dvq_ref[0] = query_grad
        aud_words = aw_ref[0, rows, :].astype(jnp.float32).astype(jnp.bfloat16)
        value_grad, key_grad, query_grad = tile_terms(
            vk, vv, aq, ag, al_ref[0, :, rows], ad_ref[0, :, rows], aud_words, 0)
        part_ref[2, 0, rows, :] = query_grad.astype(jnp.bfloat16)
        if first:
            dvk_ref[0] += key_grad
            dvv_ref[0] += value_grad
        else:
            dvk_ref[0] = key_grad
            dvv_ref[0] = value_grad


def attention(aud, vq, vk, vv, vg, vl, vd, vw, al, ad, aw):
    heads, video, width = vq.shape
    audio = aud.shape[2]
    rows = lambda a: pl.BlockSpec((1,) + a.shape[1:], lambda h: (h,) + (0,) * (a.ndim - 1))
    args = (vq, vk, vv, vg, vl, vd, vw, al, ad, aw)
    grad = jax.ShapeDtypeStruct((heads, video, width), jnp.float32)
    stack = lambda n: pl.BlockSpec((n, 1, audio, width), lambda h: (0, h, 0, 0))
    return pl.pallas_call(
        attention_kernel,
        grid=(heads,),
        out_shape=(grad, grad, grad, jax.ShapeDtypeStruct((3, heads, audio, width), jnp.bfloat16)),
        in_specs=[stack(4)] + [rows(a) for a in args],
        out_specs=(rows(vq), rows(vq), rows(vq), stack(3)),
        compiler_params=pltpu.CompilerParams(vmem_limit_bytes=48 << 20),
        name="attention_grads",
    )(aud, *args)


def square_sums(tokens):
    values = tokens.astype(jnp.float32)
    return jnp.sum(values * values, axis=(0, 2))


def normalize(tokens, scales, gain_rows):
    return (tokens.astype(jnp.float32) * scales[None, :, None] * gain_rows[:, None, :]).astype(jnp.bfloat16)


def norm_parts(tokens, scales, gain_rows, upstream):
    weighted = upstream * gain_rows[:, None, :]
    unit_rows = tokens.astype(jnp.float32) * scales[None, :, None]
    return (weighted, unit_rows, jnp.sum(weighted * unit_rows, axis=(0, 2)))


def norm_finish(weighted, unit_rows, scales, product, feature_count):
    mean_term = product / feature_count
    return (scales[None, :, None] * (weighted - unit_rows * mean_term[None, :, None])).astype(jnp.bfloat16)


def local(vid_query, vid_key, vid_value, vid_out, vid_grad, vid_lse, vid_mask, aud_query, aud_key, aud_value,
          aud_out, aud_grad, aud_lse, aud_mask, gain_vq, gain_ak, gain_aq, gain_vk):
    heads, video, width = vid_query.shape
    tokens = aud_key.shape[1]
    feature_count = lax.axis_size("head") * heads * width
    zs = lax.axis_size("ctx") // (XS * CORES)
    audio = tokens * lax.axis_size("ctx")
    sums = lax.psum(
        jnp.concatenate([square_sums(a) for a in (vid_query, vid_key, aud_query, aud_key)]), "head")
    scales = lax.rsqrt(sums / feature_count + EPS)
    scale_vq, scale_vk = scales[:video], scales[video:2 * video]
    scale_aq, scale_ak = scales[2 * video:2 * video + tokens], scales[2 * video + tokens:]
    video_delta = jnp.sum(vid_grad.astype(jnp.float32) * vid_out.astype(jnp.float32), axis=2)
    audio_delta = jnp.sum(aud_grad.astype(jnp.float32) * aud_out.astype(jnp.float32), axis=2)
    big = jnp.concatenate(
        [normalize(aud_key, scale_ak, gain_ak), aud_value, normalize(aud_query, scale_aq, gain_aq), aud_grad])
    small = jnp.pad(jnp.concatenate([aud_lse, audio_delta]), ((0, 0), (0, 128 - tokens)))
    big, small = gather(big, small, zs)
    big = big.reshape(4, heads, audio, width)
    small = small[..., :tokens].transpose(3, 0, 1, 2, 4).reshape(2, heads, 1, audio)
    up_vq, up_vk, up_vv, part = attention(
        big, normalize(vid_query, scale_vq, gain_vq), normalize(vid_key, scale_vk, gain_vk), vid_value, vid_grad,
        vid_lse[:, None], video_delta[:, None], vid_mask, small[0], small[1], aud_mask)
    sums = scatter(part.reshape(3 * heads, zs, XS, CORES, tokens, width), zs).reshape(3, heads, tokens, width)
    up_ak, up_av, up_aq = sums[0], sums[1], sums[2]
    parts = [
        norm_parts(vid_query, scale_vq, gain_vq, up_vq),
        norm_parts(vid_key, scale_vk, gain_vk, up_vk),
        norm_parts(aud_query, scale_aq, gain_aq, up_aq),
        norm_parts(aud_key, scale_ak, gain_ak, up_ak),
    ]
    product = lax.psum(jnp.concatenate([p[2] for p in parts]), "head")
    cuts = (0, video, 2 * video, 2 * video + tokens, 2 * video + 2 * tokens)
    done = [
        norm_finish(w, u, scales[lo:hi], product[lo:hi], feature_count)
        for (w, u, _), lo, hi in zip(parts, cuts[:-1], cuts[1:])
    ]
    return (done[0], done[1], up_vv.astype(jnp.bfloat16), done[2], done[3], up_av.astype(jnp.bfloat16))


def solution(mesh):
    rows = P("head", "ctx", None)
    line = P("head", "ctx")
    gain = P("head", None)
    return jax.shard_map(
        local,
        mesh=mesh,
        in_specs=(rows, rows, rows, rows, rows, line, rows, rows, rows, rows, rows, rows, line,
                  P("head", None, "ctx"), gain, gain, gain, gain),
        out_specs=(rows,) * 6,
        check_vma=False,
    )
```

time: 377 us -> 123 us (0.33)
  waiting for transfers between devices: 224 us -> 0 us
  Pallas kernels: 0 us -> 84.7 us
  matrix products: 49.7 us -> 0 us
  blocking collectives: 50.7 us -> 10.8 us
  between operations: 14.4 us -> 0.89 us
  local copies, waits for them, and re-layouts: 19.2 us -> 8.91 us
    reduce_scatter x3 -> x0, waiting for transfers between devices: 140 us -> none  [the longest x1 63.5 us: local(): lax.psum_scatter(query_partial, 'ctx', scatter_dimension=1, tiled=True)]
    pallas_call x0 -> x3, Pallas kernels: none -> 84.7 us  [the longest x1 36.2 us: gather(): pl.pallas_call(functools.partial(gather_kernel, zs), out_shape=(jax.Shape...]
    all_gather x4 -> x0, waiting for transfers between devices: 82.5 us -> none  [the longest x1 39 us: local(): grad_piece = lax.all_gather(aud_grad, 'ctx', axis=1, tiled=True)]
    dot_general x20 -> x0, matrix products: 49.7 us -> none  [the longest x8 23.3 us: dot_cols(): lax.dot_general(left, right, (((1,), (1,)), ((0,), (0,))), preferred_elem...]
    all_gather x2 -> x0, blocking collectives: 39.9 us -> none  [the longest x1 22.3 us: local(): lax.all_gather(audio_delta, 'ctx', axis=1, tiled=True)]
    shift_right_arithmetic x12 -> x0, local copies, waits for them, and re-layouts: 9.51 us -> none  [unpack_bits(): jnp.right_shift(word_rows[..., None], shifts)]
    unnamed x39 -> x37, local copies, waits for them, and re-layouts: 1.5 us -> 7.24 us
    another operation x3 -> x0, local copies, waits for them, and re-layouts: 4.38 us -> none
  transfers between devices with their start and end apart: 7 -> 0, of which waited for: 6 -> 0; matrix products, arithmetic and copies ran while one was open for 22% -> 0% of each run, Pallas kernels for 0% -> 0%
where the time goes in v1:
time: 123 us; the launch traced here: 122 us
  Pallas kernels  84.7 us (69%)
  other arithmetic  16.8 us (14%)
  blocking collectives  10.8 us (9%)
  local copies, waits for them, and re-layouts  8.91 us (7%)
    pallas_call x1, Pallas kernels, gather(): pl.pallas_call(functools.partial(gather_kernel, zs), out_shape=(jax.Shape...  36.2 us
    pallas_call x1, Pallas kernels, scatter(): pl.pallas_call(functools.partial(scatter_kernel, zs), out_shape=jax.Shape...  34.6 us
    pallas_call x1, Pallas kernels, attention(): pl.pallas_call(attention_kernel, grid=(heads,), out_shape=(grad, grad, gr...  13.9 us
    unnamed x37, local copies, waits for them, and re-layouts  7.24 us
    psum x1, blocking collectives, local(): lax.psum(jnp.concatenate([square_sums(a) for a in (vid_query, vid_key, au...  5.85 us
    convert_element_type x4, other arithmetic, normalize(): (tokens.astype(jnp.float32) * scales[None, :, None] * gain_rows[:, None,...  5.43 us
    psum x1, blocking collectives, local(): product = lax.psum(jnp.concatenate([p[2] for p in parts]), 'head')  4.93 us
    convert_element_type x3, other arithmetic, norm_finish(): (scales[None, :, None] * (weighted - unit_rows * mean_term[None, :, None]...  2.59 us

profile of v1, /device:TPU:0, one launch (start us, length us, event | category | flops | bytes accessed | tf_op | source)
XLA Modules:
  0.0 122.0 jit_solution(16218574979270147404)
XLA Ops:
  0.6 1.1 fusion.29
  1.7 1.0 multiply_reduce_fusion.1
  2.7 0.7 select_maximum_fusion.small_ref
  3.4 1.3 %fusion.11 = (f32[256]{0:T(256)S(1)}, f32[256]{0:T(256)S(1)}) fusion(bf16[4,256,128]{2,1,0:T(8,128)(2,1)} %param.18, bf16[4,256,128]{2,1,0:T(8,128)(2,1)} %param.19), kind=kLoop, calls=%fused_computation.15 | loop fusion | flops 785920 | bytes 526336 | tf_op jit(solution)/shard_map/reduce_sum | solution.py:259
  4.7 5.8 %psum.14 = f32[640]{0:T(1024)S(1)} all-reduce(f32[640]{0:T(1024)S(1)} %pad_maximum_fusion.1), channel_id=1, replica_groups=mesh['ctx'=16,'head'=2] {'head'}, use_global_device_ids=true, to_apply=%region_4.0 | all-reduce | flops 640 | bytes 5120 | tf_op jit(solution)/shard_map/psum | solution.py:284
  10.7 1.2 %multiply_reduce_fusion = f32[4,256]{1,0:T(4,128)S(1)} fusion(bf16[4,256,128]{2,1,0:T(8,128)(2,1)} %param.21, bf16[4,256,128]{2,1,0:T(8,128)(2,1)} %vg_ref.1), kind=kLoop, calls=%fused_computation.22 | loop fusion | flops 523264 | bytes 528384 | tf_op jit(solution)/shard_map/reduce_sum | solution.py:289
  11.9 0.7 broadcast_in_dim.4.vl_ref
  12.6 0.9 fusion.30
  13.5 0.9 fusion.24
  14.5 0.9 pad_maximum_fusion.big_ref
  15.4 1.8 %fusion.12.vk_ref = bf16[4,256,128]{2,1,0:T(8,128)(2,1)} fusion(bf16[4,256,128]{2,1,0:T(8,128)(2,1)} %param.19, f32[4,128]{1,0:T(4,128)} %param.35, f32[256]{0:T(256)S(1)} %get-tuple-element.28), kind=kLoop, calls=%fused_computation.16 | loop fusion | flops 524288 | bytes 527360 | tf_op jit(solution)/shard_map/convert_element_type | solution.py:263
  17.2 1.8 %fusion.6.vq_ref = bf16[4,256,128]{2,1,0:T(8,128)(2,1)} fusion(bf16[4,256,128]{2,1,0:T(8,128)(2,1)} %param.18, f32[4,128]{1,0:T(4,128)} %param.32, f32[256]{0:T(256)S(1)} %get-tuple-element.29), kind=kLoop, calls=%fused_computation.10 | loop fusion | flops 524288 | bytes 527360 | tf_op jit(solution)/shard_map/convert_element_type | solution.py:263
  19.0 0.6 copy.26.aw_ref
  19.6 36.2 %gather_audio.1 = (bf16[16,4,2,2,64,128]{5,4,3,2,1,0:T(8,128)(2,1)S(1)}, f32[4,2,2,8,128]{4,3,2,1,0:T(8,128)S(1)}) custom-call(bf16[16,64,128]{2,1,0:T(8,128)(2,1)S(1)} %pad_maximum_fusion.big_ref, f32[8,128]{1,0:T(8,128)S(1)} %select_maximum_fusion.small_ref), custom_call_target="tpu_custom_call" | custom-call | tf_op jit(solution)/shard_map/gather_audio/pallas_call | solution.py:105
  55.8 1.9 %copy-done = bf16[16,4,2,2,64,128]{5,4,3,2,1,0:T(8,128)(2,1)} copy-done((bf16[16,4,2,2,64,128]{5,4,3,2,1,0:T(8,128)(2,1)}, bf16[16,4,2,2,64,128]{5,4,3,2,1,0:T(8,128)(2,1)S(1)}, u32[]{:S(2)}) %copy-start) | copy-done | bytes 4194328
  57.9 0.1 squeeze.4.al_ref
  58.0 0.9 copy-done.2
  58.9 0.9 copy-done.3
  59.9 1.0 copy-done.4
  60.9 0.9 copy-done.7
  61.9 13.9 %attention_grads.1 = (f32[4,256,128]{2,1,0:T(8,128)S(1)}, f32[4,256,128]{2,1,0:T(8,128)S(1)}, f32[4,256,128]{2,1,0:T(8,128)S(1)}, bf16[3,4,1024,128]{3,2,1,0:T(8,128)(2,1)}) custom-call(bf16[4,4,1024,128]{3,2,1,0:T(8,128)(2,1)} %bitcast.4, bf16[4,256,128]{2,1,0:T(8,128)(2,1)S(1)} %copy-done.3, bf16[4,256,128]{2,1,0:T(8,128)(2,1)S(1)} %copy-done.2, ...), custom_call_target="tpu_custom_call" | custom-call | tf_op jit(solution)/shard_map/attention_grads/pallas_call | solution.py:246
  75.7 0.8 copy-done.5
  76.6 34.6 %scatter_audio.1 = f32[12,64,128]{2,1,0:T(8,128)} custom-call(bf16[12,4,2,2,64,128]{5,4,3,2,1,0:T(8,128)(2,1)} %bitcast.5), custom_call_target="tpu_custom_call" | custom-call | tf_op jit(solution)/shard_map/scatter_audio/pallas_call | solution.py:165
  111.3 0.2 fusion.7
  111.5 0.2 fusion.13
  111.8 1.2 fusion.25
  113.0 4.9 %psum.15 = f32[640]{0:T(1024)S(1)} all-reduce(f32[640]{0:T(1024)S(1)} %pad_maximum_fusion.2), channel_id=1, replica_groups=mesh['ctx'=16,'head'=2] {'head'}, use_global_device_ids=true, to_apply=%region_11.12 | all-reduce | flops 640 | bytes 5120 | tf_op jit(solution)/shard_map/psum | solution.py:308
  118.0 0.9 fusion.10
  118.9 0.9 fusion.16
  119.8 0.6 slice.85
  120.5 0.8 fusion.34
  121.3 0.7 convert_element_type.76
  (43 shorter events, 0.5 us)
Async XLA Ops:
  0.6 18.3 %copy-start.13 = (s32[4,1024,32]{1,2,0:T(8,128)S(1)}, s32[4,1024,32]{1,2,0:T(8,128)}, u32[]{:S(2)}) copy-start(s32[4,1024,32]{1,2,0:T(8,128)} %param.31) | copy-start | bytes 1572868
  3.4 54.6 %copy-start.1 = (bf16[4,256,128]{2,1,0:T(8,128)(2,1)S(1)}, bf16[4,256,128]{2,1,0:T(8,128)(2,1)}, u32[]{:S(2)}) copy-start(bf16[4,256,128]{2,1,0:T(8,128)(2,1)} %vg_ref.1) | copy-start | bytes 786436
  55.8 1.9 %copy-start = (bf16[16,4,2,2,64,128]{5,4,3,2,1,0:T(8,128)(2,1)}, bf16[16,4,2,2,64,128]{5,4,3,2,1,0:T(8,128)(2,1)S(1)}, u32[]{:S(2)}) copy-start(bf16[16,4,2,2,64,128]{5,4,3,2,1,0:T(8,128)(2,1)S(1)} %get-tuple-element.12) | copy-start | bytes 12582916
  58.0 1.0 copy-start.2
  58.9 0.9 copy-start.3
  59.9 1.0 copy-start.4
  60.9 0.9 copy-start.7
  75.7 0.8 copy-start.5
  76.5 34.7 %copy-start.8 = (bf16[4,256,128]{2,1,0:T(8,128)(2,1)S(1)}, bf16[4,256,128]{2,1,0:T(8,128)(2,1)}, u32[]{:S(2)}) copy-start(bf16[4,256,128]{2,1,0:T(8,128)(2,1)} %param.18) | copy-start | bytes 786436
  76.5 34.7 %copy-start.14 = (f32[4,128]{1,0:T(4,128)S(1)}, f32[4,128]{1,0:T(4,128)}, u32[]{:S(2)}) copy-start(f32[4,128]{1,0:T(4,128)} %param.32) | copy-start | bytes 6148
  76.5 35.0 %copy-start.9 = (bf16[4,256,128]{2,1,0:T(8,128)(2,1)S(1)}, bf16[4,256,128]{2,1,0:T(8,128)(2,1)}, u32[]{:S(2)}) copy-start(bf16[4,256,128]{2,1,0:T(8,128)(2,1)} %param.19) | copy-start | bytes 786436
  76.5 35.0 %copy-start.15 = (f32[4,128]{1,0:T(4,128)S(1)}, f32[4,128]{1,0:T(4,128)}, u32[]{:S(2)}) copy-start(f32[4,128]{1,0:T(4,128)} %param.35) | copy-start | bytes 6148
  76.5 35.2 %copy-start.11 = (bf16[4,64,128]{2,1,0:T(8,128)(2,1)S(1)}, bf16[4,64,128]{2,1,0:T(8,128)(2,1)}, u32[]{:S(2)}) copy-start(bf16[4,64,128]{2,1,0:T(8,128)(2,1)} %param.25) | copy-start | bytes 196612
  76.5 35.2 %copy-start.12 = (bf16[4,64,128]{2,1,0:T(8,128)(2,1)S(1)}, bf16[4,64,128]{2,1,0:T(8,128)(2,1)}, u32[]{:S(2)}) copy-start(bf16[4,64,128]{2,1,0:T(8,128)(2,1)} %param.26) | copy-start | bytes 196612
  76.6 35.2 %copy-start.16 = (f32[4,128]{1,0:T(4,128)S(1)}, f32[4,128]{1,0:T(4,128)}, u32[]{:S(2)}) copy-start(f32[4,128]{1,0:T(4,128)} %param.34) | copy-start | bytes 6148
  76.6 35.2 %copy-start.17 = (f32[4,128]{1,0:T(4,128)S(1)}, f32[4,128]{1,0:T(4,128)}, u32[]{:S(2)}) copy-start(f32[4,128]{1,0:T(4,128)} %param.33) | copy-start | bytes 6148
  111.3 8.6 %copy-start.10 = (f32[12,64,128]{2,1,0:T(8,128)S(1)}, f32[12,64,128]{2,1,0:T(8,128)}, u32[]{:S(2)}) copy-start(f32[12,64,128]{2,1,0:T(8,128)} %scatter_audio.1) | copy-start | bytes 1179652
  111.3 10.0 %copy-start.6 = (f32[4,256,128]{2,1,0:T(8,128)S(1)}, f32[4,256,128]{2,1,0:T(8,128)}, u32[]{:S(2)}) copy-start(f32[4,256,128]{2,1,0:T(8,128)} %copy-done.5) | copy-start | bytes 1572868

commit v2 on v1

v2 whole, which is shorter than its diff:
```python
import functools

import jax
import jax.numpy as jnp
from jax import lax
from jax.experimental import pallas as pl
from jax.experimental.pallas import tpu as pltpu
from jax.sharding import PartitionSpec as P

EPS = 1e-06
XS = 2
CORES = 2
MESH = pl.DeviceIdType.MESH


def place():
    me = lax.axis_index("ctx")
    return me // (XS * CORES), lax.rem(me // CORES, XS), lax.rem(me, CORES)


def peer(z, x, c):
    return {"ctx": (z * XS + x) * CORES + c}


def enter(z, x, c, zs):
    barrier = pltpu.get_barrier_semaphore()
    targets = [peer(z, x, 1 - c), peer(z, 1 - x, c)]
    targets += [peer(lax.rem(z + d, zs), x, c) for d in range(1, zs)]
    for target in targets:
        pl.semaphore_signal(barrier, inc=1, device_id=target, device_id_type=MESH)
    pl.semaphore_wait(barrier, len(targets))


def rows_dot(left, right):
    return lax.dot_general(left, right, (((1,), (1,)), ((), ())), preferred_element_type=jnp.float32)


def cols_dot(left, right):
    return lax.dot_general(left, right, (((0,), (0,)), ((), ())), preferred_element_type=jnp.float32)


def plain_dot(left, right):
    return lax.dot_general(left, right, (((1,), (0,)), ((), ())), preferred_element_type=jnp.float32)


def tile_terms(keys, values, queries, grads, lse, delta, words, first_key):
    nk, nw = keys.shape[0], words.shape[1]
    scale = keys.shape[1] ** (-0.5)
    key_of = lax.broadcasted_iota(jnp.int32, (nk, nw), 0) + first_key
    word_of = lax.broadcasted_iota(jnp.int32, (nk, nw), 1)
    spread = jnp.where(key_of // 8 == word_of, 1.0, 0.0).astype(jnp.bfloat16)
    spread_words = rows_dot(spread, words).astype(jnp.int32)
    shape = spread_words.shape
    bit = jnp.left_shift(1, lax.rem(lax.broadcasted_iota(jnp.int32, shape, 0), 8))
    keep = jnp.bitwise_and(spread_words, bit) != 0
    probs = jnp.exp(rows_dot(keys, queries) * scale - lse)
    dropped = jnp.where(keep, 2.0 * probs, 0.0).astype(jnp.bfloat16)
    prob_grad = jnp.where(keep, 2.0 * rows_dot(values, grads), 0.0)
    score_grad = (probs * (prob_grad - delta)).astype(jnp.bfloat16)
    return (
        plain_dot(dropped, grads),
        scale * plain_dot(score_grad, queries),
        scale * cols_dot(score_grad, keys),
    )


def fused_kernel(zs, big_ref, small_ref, vq_ref, vk_ref, vv_ref, vg_ref, vl_ref, vd_ref, vw_ref, aw_ref,
                 dvq_ref, dvk_ref, dvv_ref, sum_ref,
                 big_out, small_out, part, core_in, x_out, x_in, z_out, z_in,
                 z_send, z_recv, x_send, x_recv, c_send, c_recv, own_sem,
                 pc_send, pc_recv, px_send, px_recv, pz_send, pz_recv):
    z, x, c = place()
    heads = vq_ref.shape[0]
    width = vq_ref.shape[2]
    chunk = XS * CORES * big_ref.shape[1]
    source = [lax.rem(z + zs - d, zs) for d in range(zs)]
    enter(z, x, c, zs)
    pairs = ((big_ref, big_out), (small_ref, small_out))

    def slot(k, zz, xx):
        out = pairs[k][1]
        return out.at[:, zz, xx, c] if k == 0 else out.at[zz, xx, c]

    def copies(here, there, send, recv, target):
        return [pltpu.make_async_remote_copy(
            src_ref=here(k), dst_ref=there(k), send_sem=send(k), recv_sem=recv(k), device_id=target,
            device_id_type=MESH) for k in range(2)]

    own_src = lambda k: pairs[k][0]
    z_copies, x_copies, c_copies = [None], [], [[], []]
    for d in range(zs):
        mine = lambda k, d=d: slot(k, source[d], x)
        other = lambda k, d=d: slot(k, source[d], 1 - x)
        src = mine if d else own_src
        if d:
            z_copies.append(copies(own_src, lambda k: slot(k, z, x), lambda k, d=d: z_send.at[k, d],
                                   lambda k, d=d: z_recv.at[k, d], peer(lax.rem(z + d, zs), x, c)))
        x_copies.append(copies(src, mine, lambda k, d=d: x_send.at[k, d], lambda k, d=d: x_recv.at[k, d],
                               peer(z, 1 - x, c)))
        for side, here, there in ((0, src, mine), (1, other, other)):
            c_copies[side].append(copies(here, there, lambda k, d=d, side=side: c_send.at[k, d, side],
                                         lambda k, d=d, side=side: c_recv.at[k, d, side], peer(z, x, 1 - c)))
    own = [pltpu.make_async_copy(pairs[k][0], slot(k, z, x), own_sem.at[k]) for k in range(2)]
    pc_copies = [pltpu.make_async_remote_copy(
        src_ref=part.at[d, :, :, 1 - c], dst_ref=core_in.at[d], send_sem=pc_send.at[d], recv_sem=pc_recv.at[d],
        device_id=peer(z, x, 1 - c), device_id_type=MESH) for d in range(zs)]
    px_copies = [pltpu.make_async_remote_copy(
        src_ref=x_out.at[d], dst_ref=x_in.at[d], send_sem=px_send.at[d], recv_sem=px_recv.at[d],
        device_id=peer(z, 1 - x, c), device_id_type=MESH) for d in range(zs)]
    pz_copies = [None] + [pltpu.make_async_remote_copy(
        src_ref=z_out.at[d], dst_ref=z_in.at[d], send_sem=pz_send.at[d], recv_sem=pz_recv.at[d],
        device_id=peer(source[d], x, c), device_id_type=MESH) for d in range(1, zs)]

    def start(group):
        for copy in group:
            copy.start()

    def arrive(group):
        for copy in group:
            copy.wait_recv()

    def left(group):
        for copy in group:
            copy.wait_send()

    def compute(d):
        zz = source[d]
        rows = pl.ds(pl.multiple_of(zz * chunk, chunk), chunk)

        def head(h, carry):
            ak, av, aq, ag = (big_out[i * heads + h, zz].reshape(chunk, width) for i in range(4))
            lines = lambda i: sum(
                small_out[zz, xx, cc, pl.ds(i * heads + h, 1), :] for xx in range(XS) for cc in range(CORES))
            value_grad, key_grad, query_grad = tile_terms(
                ak, av, vq_ref[h], vg_ref[h], vl_ref[h], vd_ref[h],
                vw_ref[h].astype(jnp.float32).astype(jnp.bfloat16), zz * chunk)
            aud_words = aw_ref[h, rows, :].astype(jnp.float32).astype(jnp.bfloat16)
            vid_value_grad, vid_key_grad, aud_query_grad = tile_terms(
                vk_ref[h], vv_ref[h], aq, ag, lines(0), lines(1), aud_words, 0)
            for i, total in enumerate((key_grad, value_grad, aud_query_grad)):
                part[d, i * heads + h] = total.astype(part.dtype).reshape(part.shape[2:])
            if d:
                dvq_ref[h] += query_grad
                dvk_ref[h] += vid_key_grad
                dvv_ref[h] += vid_value_grad
            else:
                dvq_ref[h] = query_grad
                dvk_ref[h] = vid_key_grad
                dvv_ref[h] = vid_value_grad
            return carry

        lax.fori_loop(0, heads, head, 0)

    def core_sum(d, side):
        return part[d, :, side, c].astype(jnp.float32) + core_in[d, :, side].astype(jnp.float32)

    def to_x(d):
        pc_copies[d].wait_recv()
        x_out[d] = core_sum(d, 1 - x).astype(x_out.dtype)
        px_copies[d].start()

    def to_z(d):
        px_copies[d].wait_recv()
        both = core_sum(d, x) + x_in[d].astype(jnp.float32)
        if d:
            z_out[d] = both.astype(z_out.dtype)
            pz_copies[d].start()
        else:
            sum_ref[...] = both

    start(z_copies[1])
    start(x_copies[0])
    start(c_copies[0][0])
    start(own)
    for copy in own:
        copy.wait()
    for d in range(zs):
        if d + 1 < zs:
            if d + 2 < zs:
                left(z_copies[d + 1])
                start(z_copies[d + 2])
            arrive(z_copies[d + 1])
            start(x_copies[d + 1])
            start(c_copies[0][d + 1])
        arrive(x_copies[d])
        start(c_copies[1][d])
        if d > 0:
            to_x(d - 1)
        if d > 1:
            to_z(d - 2)
        arrive(c_copies[0][d])
        arrive(c_copies[1][d])
        compute(d)
        pc_copies[d].start()
    to_x(zs - 1)
    for d in range(max(zs - 2, 0), zs):
        to_z(d)
    for d in range(1, zs):
        pz_copies[d].wait_recv()
        sum_ref[...] += z_in[d].astype(jnp.float32)
    left(z_copies[zs - 1])
    for d in range(zs):
        left(x_copies[d])
        left(c_copies[0][d])
        left(c_copies[1][d])
        pc_copies[d].wait_send()
        px_copies[d].wait_send()
        if d:
            pz_copies[d].wait_send()


def fused(zs, big, small, vq, vk, vv, vg, vl, vd, vw, aw):
    rows, tokens, width = big.shape
    heads = vq.shape[0]
    lines = 3 * heads
    sems = lambda *shape: pltpu.SemaphoreType.DMA(shape)
    block = lambda *lead: pltpu.VMEM((zs, lines) + lead + (tokens, width), jnp.bfloat16)
    grad = jax.ShapeDtypeStruct(vq.shape, jnp.float32)
    vmem = pl.BlockSpec(memory_space=pltpu.VMEM)
    return pl.pallas_call(
        functools.partial(fused_kernel, zs),
        out_shape=(grad, grad, grad, jax.ShapeDtypeStruct((lines, tokens, width), jnp.float32)),
        in_specs=[vmem] * 10,
        out_specs=[vmem] * 4,
        scratch_shapes=[
            pltpu.VMEM((rows, zs, XS, CORES, tokens, width), big.dtype),
            pltpu.VMEM((zs, XS, CORES) + small.shape, small.dtype),
            block(XS, CORES), block(XS), block(), block(), block(), block(),
            sems(2, zs), sems(2, zs), sems(2, zs), sems(2, zs), sems(2, zs, 2), sems(2, zs, 2), sems(2),
        ] + [sems(zs) for _ in range(6)],
        compiler_params=pltpu.CompilerParams(collective_id=0, has_side_effects=True, vmem_limit_bytes=56 << 20),
        name="fused_grads",
    )(big, small, vq, vk, vv, vg, vl, vd, vw, aw)


def square_sums(tokens):
    values = tokens.astype(jnp.float32)
    return jnp.sum(values * values, axis=(0, 2))


def normalize(tokens, scales, gain_rows):
    return (tokens.astype(jnp.float32) * scales[None, :, None] * gain_rows[:, None, :]).astype(jnp.bfloat16)


def norm_parts(tokens, scales, gain_rows, upstream):
    weighted = upstream * gain_rows[:, None, :]
    unit_rows = tokens.astype(jnp.float32) * scales[None, :, None]
    return (weighted, unit_rows, jnp.sum(weighted * unit_rows, axis=(0, 2)))


def norm_finish(weighted, unit_rows, scales, product, feature_count):
    mean_term = product / feature_count
    return (scales[None, :, None] * (weighted - unit_rows * mean_term[None, :, None])).astype(jnp.bfloat16)


def local(vid_query, vid_key, vid_value, vid_out, vid_grad, vid_lse, vid_mask, aud_query, aud_key, aud_value,
          aud_out, aud_grad, aud_lse, aud_mask, gain_vq, gain_ak, gain_aq, gain_vk):
    heads, video, width = vid_query.shape
    tokens = aud_key.shape[1]
    feature_count = lax.axis_size("head") * heads * width
    zs = lax.axis_size("ctx") // (XS * CORES)
    sums = lax.psum(
        jnp.concatenate([square_sums(a) for a in (vid_query, vid_key, aud_query, aud_key)]), "head")
    scales = lax.rsqrt(sums / feature_count + EPS)
    scale_vq, scale_vk = scales[:video], scales[video:2 * video]
    scale_aq, scale_ak = scales[2 * video:2 * video + tokens], scales[2 * video + tokens:]
    video_delta = jnp.sum(vid_grad.astype(jnp.float32) * vid_out.astype(jnp.float32), axis=2)
    audio_delta = jnp.sum(aud_grad.astype(jnp.float32) * aud_out.astype(jnp.float32), axis=2)
    big = jnp.concatenate(
        [normalize(aud_key, scale_ak, gain_ak), aud_value, normalize(aud_query, scale_aq, gain_aq), aud_grad])
    near = XS * CORES
    lane_owner = jnp.arange(near * tokens) // tokens
    small = jnp.where(
        lane_owner[None] == lax.rem(lax.axis_index("ctx"), near),
        jnp.tile(jnp.concatenate([aud_lse, audio_delta]), (1, near)), 0.0)
    up_vq, up_vk, up_vv, sums = fused(
        zs, big, small, normalize(vid_query, scale_vq, gain_vq), normalize(vid_key, scale_vk, gain_vk), vid_value,
        vid_grad, vid_lse[:, None], video_delta[:, None], vid_mask, aud_mask)
    sums = sums.reshape(3, heads, tokens, width)
    up_ak, up_av, up_aq = sums[0], sums[1], sums[2]
    parts = [
        norm_parts(vid_query, scale_vq, gain_vq, up_vq),
        norm_parts(vid_key, scale_vk, gain_vk, up_vk),
        norm_parts(aud_query, scale_aq, gain_aq, up_aq),
        norm_parts(aud_key, scale_ak, gain_ak, up_ak),
    ]
    product = lax.psum(jnp.concatenate([p[2] for p in parts]), "head")
    cuts = (0, video, 2 * video, 2 * video + tokens, 2 * video + 2 * tokens)
    done = [
        norm_finish(w, u, scales[lo:hi], product[lo:hi], feature_count)
        for (w, u, _), lo, hi in zip(parts, cuts[:-1], cuts[1:])
    ]
    return (done[0], done[1], up_vv.astype(jnp.bfloat16), done[2], done[3], up_av.astype(jnp.bfloat16))


def solution(mesh):
    rows = P("head", "ctx", None)
    line = P("head", "ctx")
    gain = P("head", None)
    return jax.shard_map(
        local,
        mesh=mesh,
        in_specs=(rows, rows, rows, rows, rows, line, rows, rows, rows, rows, rows, rows, line,
                  P("head", None, "ctx"), gain, gain, gain, gain),
        out_specs=(rows,) * 6,
        check_vma=False,
    )
```

time: 123 us -> 104 us (0.85)
  Pallas kernels: 84.7 us -> 68.4 us
  local copies, waits for them, and re-layouts: 8.91 us -> 4.71 us
  other arithmetic: 16.8 us -> 18.4 us
    pallas_call x3 -> x1, Pallas kernels: 84.7 us -> 68.4 us  [fused(): pl.pallas_call(functools.partial(fused_kernel, zs), out_shape=(grad, grad...]
    unnamed x37 -> x25, local copies, waits for them, and re-layouts: 7.24 us -> 2.02 us
    convert_element_type x4, other arithmetic: 5.43 us -> 3.53 us  [normalize(): (tokens.astype(jnp.float32) * scales[None, :, None] * gain_rows[:, None,...]
where the time goes in v2:
time: 104 us; the launch traced here: 103 us
  Pallas kernels  68.4 us (66%)
  other arithmetic  18.4 us (18%)
  blocking collectives  10.8 us (10%)
  local copies, waits for them, and re-layouts  4.71 us (5%)
    pallas_call x1, Pallas kernels, fused(): pl.pallas_call(functools.partial(fused_kernel, zs), out_shape=(grad, grad...  68.4 us
    psum x1, blocking collectives, local(): lax.psum(jnp.concatenate([square_sums(a) for a in (vid_query, vid_key, au...  5.85 us
    psum x1, blocking collectives, local(): product = lax.psum(jnp.concatenate([p[2] for p in parts]), 'head')  4.92 us
    convert_element_type x4, other arithmetic, normalize(): (tokens.astype(jnp.float32) * scales[None, :, None] * gain_rows[:, None,...  3.53 us
    reduce_sum x3, other arithmetic, norm_parts(): return (weighted, unit_rows, jnp.sum(weighted * unit_rows, axis=(0, 2)))  2.71 us
    convert_element_type x3, other arithmetic, norm_finish(): (scales[None, :, None] * (weighted - unit_rows * mean_term[None, :, None]...  2.59 us
    reduce_sum x2, other arithmetic, square_sums(): return jnp.sum(values * values, axis=(0, 2))  2.28 us

profile of v2, /device:TPU:0, one launch (start us, length us, event | category | flops | bytes accessed | tf_op | source)
XLA Modules:
  0.0 103.1 jit_solution(7984737269103348638)
XLA Ops:
  0.6 0.0 copy-start.1
  0.7 1.1 %fusion.29 = (f32[64]{0:T(128)S(1)}, f32[64]{0:T(128)S(1)}) fusion(bf16[4,64,128]{2,1,0:T(8,128)(2,1)} %param.25, bf16[4,64,128]{2,1,0:T(8,128)(2,1)} %param.26), kind=kLoop, calls=%fused_computation.39 | loop fusion | flops 196480 | bytes 131584 | tf_op jit(solution)/shard_map/reduce_sum | solution.py:238
  1.8 1.0 multiply_reduce_fusion.1
  2.8 0.7 pad_maximum_fusion.2
  3.5 1.2 %fusion.11 = (f32[256]{0:T(256)S(1)}, f32[256]{0:T(256)S(1)}) fusion(bf16[4,256,128]{2,1,0:T(8,128)(2,1)} %param.18, bf16[4,256,128]{2,1,0:T(8,128)(2,1)} %param.19), kind=kLoop, calls=%fused_computation.15 | loop fusion | flops 785920 | bytes 526336 | tf_op jit(solution)/shard_map/reduce_sum | solution.py:238
  4.7 0.1 pad_maximum_fusion.1
  4.8 5.8 %psum.14 = f32[640]{0:T(1024)S(1)} all-reduce(f32[640]{0:T(1024)S(1)} %pad_maximum_fusion.1), channel_id=1, replica_groups=mesh['ctx'=16,'head'=2] {'head'}, use_global_device_ids=true, to_apply=%region_4.0 | all-reduce | flops 640 | bytes 5120 | tf_op jit(solution)/shard_map/psum | solution.py:262
  10.6 0.1 fusion.38
  10.7 1.2 %multiply_reduce_fusion = f32[4,256]{1,0:T(4,128)S(1)} fusion(bf16[4,256,128]{2,1,0:T(8,128)(2,1)} %param.21, bf16[4,256,128]{2,1,0:T(8,128)(2,1)} %vg_ref.1), kind=kLoop, calls=%fused_computation.22 | loop fusion | flops 523264 | bytes 528384 | tf_op jit(solution)/shard_map/reduce_sum | solution.py:267
  11.9 0.6 broadcast_in_dim.19.vd_ref
  12.5 1.3 %broadcast_in_dim.18.vl_ref = f32[4,1,256]{2,1,0:T(1,128)} reshape(f32[4,256]{1,0:T(4,128)} %param.23) | data formatting | bytes 8192 | tf_op jit(solution)/shard_map/broadcast_in_dim | solution.py:278
  13.8 0.1 tile.10
  13.9 0.6 broadcast_select_fusion.small_ref
  14.5 0.9 fusion.30
  15.5 0.9 fusion.24
  16.4 1.6 %pad_maximum_fusion.big_ref = bf16[16,64,128]{2,1,0:T(8,128)(2,1)} fusion(bf16[4,64,128]{2,1,0:T(8,128)(2,1)} %param.29, bf16[4,64,128]{2,1,0:T(8,128)(2,1)S(1)} %fusion.24, bf16[4,64,128]{2,1,0:T(8,128)(2,1)} %param.27, bf16[4,64,128]{2,1,0:T(8,128)(2,1)S(1)} %fusion.30), kind=kLoop, calls=%fused_computation.23 | loop fusion | flops 393216 | bytes 524288 | tf_op jit(solution)/shard_map/concatenate | solution.py:269
  18.0 0.8 fusion.12.vk_ref
  18.8 0.8 fusion.6.vq_ref
  19.7 2.0 %copy.24.aw_ref = s32[4,1024,32]{2,1,0:T(8,128)} copy(s32[4,1024,32]{1,2,0:T(8,128)S(1)} %copy-done.7) | data formatting | bytes 1048576 | tf_op args[13]
  21.6 68.4 %fused_grads.1 = (f32[4,256,128]{2,1,0:T(8,128)}, f32[4,256,128]{2,1,0:T(8,128)}, f32[4,256,128]{2,1,0:T(8,128)}, f32[12,64,128]{2,1,0:T(8,128)}) custom-call(bf16[16,64,128]{2,1,0:T(8,128)(2,1)} %pad_maximum_fusion.big_ref, f32[8,256]{1,0:T(8,128)} %broadcast_select_fusion.small_ref, bf16[4,256,128]{2,1,0:T(8,128)(2,1)} %fusion.6.vq_ref, ...), custom_call_target="tpu_custom_call" | custom-call | tf_op jit(solution)/shard_map/fused_grads/pallas_call | solution.py:220
  90.1 0.0 copy-start.5
  90.2 1.9 %convert_element_type.74 = bf16[4,256,128]{2,1,0:T(8,128)(2,1)} convert(f32[4,256,128]{2,1,0:T(8,128)} %get-tuple-element.13) | non-fusion elementwise | flops 131072 | bytes 786432 | tf_op jit(solution)/shard_map/convert_element_type | solution.py:293
  92.1 1.3 %fusion.7 = f32[256]{0:T(256)S(1)} fusion(bf16[4,256,128]{2,1,0:T(8,128)(2,1)S(1)} %copy-done, f32[4,256,128]{2,1,0:T(8,128)} %get-tuple-element.10, f32[4,128]{1,0:T(4,128)S(1)} %copy-done.8, f32[256]{0:T(256)S(1)} %get-tuple-element.23), kind=kLoop, calls=%fused_computation.11 | loop fusion | flops 655104 | bytes 790528 | tf_op jit(solution)/shard_map/reduce_sum | solution.py:248
  93.3 1.3 %fusion.13 = f32[256]{0:T(256)S(1)} fusion(bf16[4,256,128]{2,1,0:T(8,128)(2,1)S(1)} %copy-done.1, f32[4,256,128]{2,1,0:T(8,128)} %get-tuple-element.11, f32[4,128]{1,0:T(4,128)S(1)} %copy-done.9, f32[256]{0:T(256)S(1)} %get-tuple-element.22), kind=kLoop, calls=%fused_computation.17 | loop fusion | flops 655104 | bytes 790528 | tf_op jit(solution)/shard_map/reduce_sum | solution.py:248
  94.6 0.2 fusion.25
  94.8 0.1 pad_maximum_fusion.3
  94.9 4.9 %psum.15 = f32[640]{0:T(1024)S(1)} all-reduce(f32[640]{0:T(1024)S(1)} %pad_maximum_fusion.3), channel_id=1, replica_groups=mesh['ctx'=16,'head'=2] {'head'}, use_global_device_ids=true, to_apply=%region_11.12 | all-reduce | flops 640 | bytes 5120 | tf_op jit(solution)/shard_map/psum | solution.py:287
  99.8 0.1 slice_multiply_fusion.4
  99.9 0.9 fusion.10
  100.8 0.9 fusion.16
  101.7 0.6 slice.68
  102.3 0.8 fusion.34
  (27 shorter events, 0.1 us)
Async XLA Ops:
  0.6 17.4 %copy-start.1 = (bf16[4,256,128]{2,1,0:T(8,128)(2,1)S(1)}, bf16[4,256,128]{2,1,0:T(8,128)(2,1)}, u32[]{:S(2)}) copy-start(bf16[4,256,128]{2,1,0:T(8,128)(2,1)} %param.19) | copy-start | bytes 786436
  0.6 18.2 %copy-start = (bf16[4,256,128]{2,1,0:T(8,128)(2,1)S(1)}, bf16[4,256,128]{2,1,0:T(8,128)(2,1)}, u32[]{:S(2)}) copy-start(bf16[4,256,128]{2,1,0:T(8,128)(2,1)} %param.18) | copy-start | bytes 786436
  0.7 17.3 %copy-start.9 = (f32[4,128]{1,0:T(4,128)S(1)}, f32[4,128]{1,0:T(4,128)}, u32[]{:S(2)}) copy-start(f32[4,128]{1,0:T(4,128)} %param.35) | copy-start | bytes 6148
  0.7 18.2 %copy-start.8 = (f32[4,128]{1,0:T(4,128)S(1)}, f32[4,128]{1,0:T(4,128)}, u32[]{:S(2)}) copy-start(f32[4,128]{1,0:T(4,128)} %param.32) | copy-start | bytes 6148
  0.7 19.0 %copy-start.7 = (s32[4,1024,32]{1,2,0:T(8,128)S(1)}, s32[4,1024,32]{1,2,0:T(8,128)}, u32[]{:S(2)}) copy-start(s32[4,1024,32]{1,2,0:T(8,128)} %param.31) | copy-start | bytes 1572868
  90.1 4.5 %copy-start.4 = (bf16[4,64,128]{2,1,0:T(8,128)(2,1)S(1)}, bf16[4,64,128]{2,1,0:T(8,128)(2,1)}, u32[]{:S(2)}) copy-start(bf16[4,64,128]{2,1,0:T(8,128)(2,1)} %param.25) | copy-start | bytes 196612
  90.1 4.5 %copy-start.5 = (bf16[4,64,128]{2,1,0:T(8,128)(2,1)S(1)}, bf16[4,64,128]{2,1,0:T(8,128)(2,1)}, u32[]{:S(2)}) copy-start(bf16[4,64,128]{2,1,0:T(8,128)(2,1)} %param.26) | copy-start | bytes 196612
  90.1 4.5 %copy-start.6 = (f32[12,64,128]{2,1,0:T(8,128)S(1)}, f32[12,64,128]{2,1,0:T(8,128)}, u32[]{:S(2)}) copy-start(f32[12,64,128]{2,1,0:T(8,128)} %get-tuple-element.12) | copy-start | bytes 1179652
  90.1 4.5 %copy-start.10 = (f32[4,128]{1,0:T(4,128)S(1)}, f32[4,128]{1,0:T(4,128)}, u32[]{:S(2)}) copy-start(f32[4,128]{1,0:T(4,128)} %param.34) | copy-start | bytes 6148
  90.1 4.5 %copy-start.11 = (f32[4,128]{1,0:T(4,128)S(1)}, f32[4,128]{1,0:T(4,128)}, u32[]{:S(2)}) copy-start(f32[4,128]{1,0:T(4,128)} %param.33) | copy-start | bytes 6148
  90.1 9.8 %copy-start.3 = (f32[4,256,128]{2,1,0:T(8,128)S(1)}, f32[4,256,128]{2,1,0:T(8,128)}, u32[]{:S(2)}) copy-start(f32[4,256,128]{2,1,0:T(8,128)} %get-tuple-element.10) | copy-start | bytes 1572868
  90.2 10.6 %copy-start.2 = (f32[4,256,128]{2,1,0:T(8,128)S(1)}, f32[4,256,128]{2,1,0:T(8,128)}, u32[]{:S(2)}) copy-start(f32[4,256,128]{2,1,0:T(8,128)} %get-tuple-element.11) | copy-start | bytes 1572868

commit v3 on v2

--- a/solution.py
+++ b/solution.py
@@ -174,27 +174,30 @@
     start(own)
     for copy in own:
         copy.wait()
+
+    def bring(d):
+        if d + 1 < zs:
+            left(z_copies[d])
+            start(z_copies[d + 1])
+        arrive(z_copies[d])
+        start(x_copies[d])
+        start(c_copies[0][d])
+
     for d in range(zs):
-        if d + 1 < zs:
-            if d + 2 < zs:
-                left(z_copies[d + 1])
-                start(z_copies[d + 2])
-            arrive(z_copies[d + 1])
-            start(x_copies[d + 1])
-            start(c_copies[0][d + 1])
+        if 0 < d < zs - 1:
+            bring(d + 1)
         arrive(x_copies[d])
         start(c_copies[1][d])
-        if d > 0:
-            to_x(d - 1)
-        if d > 1:
-            to_z(d - 2)
         arrive(c_copies[0][d])
         arrive(c_copies[1][d])
         compute(d)
         pc_copies[d].start()
-    to_x(zs - 1)
-    for d in range(max(zs - 2, 0), zs):
-        to_z(d)
+        if d == 0:
+            bring(1)
+        to_x(d)
+        if d > 0:
+            to_z(d - 1)
+    to_z(zs - 1)
     for d in range(1, zs):
         pz_copies[d].wait_recv()
         sum_ref[...] += z_in[d].astype(jnp.float32)

time: 104 us -> 111 us (1.067)
  Pallas kernels: 68.4 us -> 76 us
    pallas_call x1, Pallas kernels: 68.4 us -> 76 us  [fused(): pl.pallas_call(functools.partial(fused_kernel, zs), out_shape=(grad, grad...]
where the time goes in v3:
time: 111 us
  Pallas kernels  76 us (68%)
  other arithmetic  18.4 us (17%)
  blocking collectives  10.8 us (10%)
  local copies, waits for them, and re-layouts  4.71 us (4%)
    pallas_call x1, Pallas kernels, fused(): pl.pallas_call(functools.partial(fused_kernel, zs), out_shape=(grad, grad...  76 us
    psum x1, blocking collectives, local(): lax.psum(jnp.concatenate([square_sums(a) for a in (vid_query, vid_key, au...  5.85 us
    psum x1, blocking collectives, local(): product = lax.psum(jnp.concatenate([p[2] for p in parts]), 'head')  4.92 us
    convert_element_type x4, other arithmetic, normalize(): (tokens.astype(jnp.float32) * scales[None, :, None] * gain_rows[:, None,...  3.53 us
    reduce_sum x3, other arithmetic, norm_parts(): return (weighted, unit_rows, jnp.sum(weighted * unit_rows, axis=(0, 2)))  2.71 us
    convert_element_type x3, other arithmetic, norm_finish(): (scales[None, :, None] * (weighted - unit_rows * mean_term[None, :, None]...  2.59 us
    reduce_sum x2, other arithmetic, square_sums(): return jnp.sum(values * values, axis=(0, 2))  2.28 us

profile of v3, /device:TPU:0, one launch (start us, length us, event | category | flops | bytes accessed | tf_op | source)
XLA Modules:
  0.0 110.7 jit_solution(1691554299470464705)
XLA Ops:
  0.6 0.0 copy-start.1
  0.7 1.1 fusion.29
  1.8 1.0 multiply_reduce_fusion.1
  2.8 0.7 pad_maximum_fusion.2
  3.5 1.2 %fusion.11 = (f32[256]{0:T(256)S(1)}, f32[256]{0:T(256)S(1)}) fusion(bf16[4,256,128]{2,1,0:T(8,128)(2,1)} %param.18, bf16[4,256,128]{2,1,0:T(8,128)(2,1)} %param.19), kind=kLoop, calls=%fused_computation.15 | loop fusion | flops 785920 | bytes 526336 | tf_op jit(solution)/shard_map/reduce_sum | solution.py:241
  4.7 0.1 pad_maximum_fusion.1
  4.8 5.8 %psum.14 = f32[640]{0:T(1024)S(1)} all-reduce(f32[640]{0:T(1024)S(1)} %pad_maximum_fusion.1), channel_id=1, replica_groups=mesh['ctx'=16,'head'=2] {'head'}, use_global_device_ids=true, to_apply=%region_4.0 | all-reduce | flops 640 | bytes 5120 | tf_op jit(solution)/shard_map/psum | solution.py:265
  10.6 0.1 fusion.38
  10.7 1.2 %multiply_reduce_fusion = f32[4,256]{1,0:T(4,128)S(1)} fusion(bf16[4,256,128]{2,1,0:T(8,128)(2,1)} %param.21, bf16[4,256,128]{2,1,0:T(8,128)(2,1)} %vg_ref.1), kind=kLoop, calls=%fused_computation.22 | loop fusion | flops 523264 | bytes 528384 | tf_op jit(solution)/shard_map/reduce_sum | solution.py:270
  11.9 0.6 broadcast_in_dim.19.vd_ref
  12.5 1.3 %broadcast_in_dim.18.vl_ref = f32[4,1,256]{2,1,0:T(1,128)} reshape(f32[4,256]{1,0:T(4,128)} %param.23) | data formatting | bytes 8192 | tf_op jit(solution)/shard_map/broadcast_in_dim | solution.py:281
  13.8 0.1 tile.10
  13.9 0.6 broadcast_select_fusion.small_ref
  14.5 0.9 fusion.30
  15.5 0.9 fusion.24
  16.4 1.6 %pad_maximum_fusion.big_ref = bf16[16,64,128]{2,1,0:T(8,128)(2,1)} fusion(bf16[4,64,128]{2,1,0:T(8,128)(2,1)} %param.29, bf16[4,64,128]{2,1,0:T(8,128)(2,1)S(1)} %fusion.24, bf16[4,64,128]{2,1,0:T(8,128)(2,1)} %param.27, bf16[4,64,128]{2,1,0:T(8,128)(2,1)S(1)} %fusion.30), kind=kLoop, calls=%fused_computation.23 | loop fusion | flops 393216 | bytes 524288 | tf_op jit(solution)/shard_map/concatenate | solution.py:272
  18.0 0.8 fusion.12.vk_ref
  18.8 0.8 fusion.6.vq_ref
  19.7 2.0 %copy.24.aw_ref = s32[4,1024,32]{2,1,0:T(8,128)} copy(s32[4,1024,32]{1,2,0:T(8,128)S(1)} %copy-done.7) | data formatting | bytes 1048576 | tf_op args[13]
  21.6 76.0 %fused_grads.1 = (f32[4,256,128]{2,1,0:T(8,128)}, f32[4,256,128]{2,1,0:T(8,128)}, f32[4,256,128]{2,1,0:T(8,128)}, f32[12,64,128]{2,1,0:T(8,128)}) custom-call(bf16[16,64,128]{2,1,0:T(8,128)(2,1)} %pad_maximum_fusion.big_ref, f32[8,256]{1,0:T(8,128)} %broadcast_select_fusion.small_ref, bf16[4,256,128]{2,1,0:T(8,128)(2,1)} %fusion.6.vq_ref, ...), custom_call_target="tpu_custom_call" | custom-call | tf_op jit(solution)/shard_map/fused_grads/pallas_call | solution.py:223
  97.7 0.0 copy-start.5
  97.8 1.9 %convert_element_type.74 = bf16[4,256,128]{2,1,0:T(8,128)(2,1)} convert(f32[4,256,128]{2,1,0:T(8,128)} %get-tuple-element.13) | non-fusion elementwise | flops 131072 | bytes 786432 | tf_op jit(solution)/shard_map/convert_element_type | solution.py:296
  99.6 1.3 %fusion.7 = f32[256]{0:T(256)S(1)} fusion(bf16[4,256,128]{2,1,0:T(8,128)(2,1)S(1)} %copy-done, f32[4,256,128]{2,1,0:T(8,128)} %get-tuple-element.10, f32[4,128]{1,0:T(4,128)S(1)} %copy-done.8, f32[256]{0:T(256)S(1)} %get-tuple-element.23), kind=kLoop, calls=%fused_computation.11 | loop fusion | flops 655104 | bytes 790528 | tf_op jit(solution)/shard_map/reduce_sum | solution.py:251
  100.9 1.3 %fusion.13 = f32[256]{0:T(256)S(1)} fusion(bf16[4,256,128]{2,1,0:T(8,128)(2,1)S(1)} %copy-done.1, f32[4,256,128]{2,1,0:T(8,128)} %get-tuple-element.11, f32[4,128]{1,0:T(4,128)S(1)} %copy-done.9, f32[256]{0:T(256)S(1)} %get-tuple-element.22), kind=kLoop, calls=%fused_computation.17 | loop fusion | flops 655104 | bytes 790528 | tf_op jit(solution)/shard_map/reduce_sum | solution.py:251
  102.2 0.2 fusion.25
  102.4 0.1 pad_maximum_fusion.3
  102.5 4.9 %psum.15 = f32[640]{0:T(1024)S(1)} all-reduce(f32[640]{0:T(1024)S(1)} %pad_maximum_fusion.3), channel_id=1, replica_groups=mesh['ctx'=16,'head'=2] {'head'}, use_global_device_ids=true, to_apply=%region_11.12 | all-reduce | flops 640 | bytes 5120 | tf_op jit(solution)/shard_map/psum | solution.py:290
  107.4 0.1 slice_multiply_fusion.4
  107.5 0.9 fusion.10
  108.4 0.9 fusion.16
  109.3 0.6 slice.68
  109.9 0.8 fusion.34
  (27 shorter events, 0.1 us)
Async XLA Ops:
  0.6 17.4 %copy-start.1 = (bf16[4,256,128]{2,1,0:T(8,128)(2,1)S(1)}, bf16[4,256,128]{2,1,0:T(8,128)(2,1)}, u32[]{:S(2)}) copy-start(bf16[4,256,128]{2,1,0:T(8,128)(2,1)} %param.19) | copy-start | bytes 786436
  0.6 18.2 %copy-start = (bf16[4,256,128]{2,1,0:T(8,128)(2,1)S(1)}, bf16[4,256,128]{2,1,0:T(8,128)(2,1)}, u32[]{:S(2)}) copy-start(bf16[4,256,128]{2,1,0:T(8,128)(2,1)} %param.18) | copy-start | bytes 786436
  0.7 17.3 %copy-start.9 = (f32[4,128]{1,0:T(4,128)S(1)}, f32[4,128]{1,0:T(4,128)}, u32[]{:S(2)}) copy-start(f32[4,128]{1,0:T(4,128)} %param.35) | copy-start | bytes 6148
  0.7 18.2 %copy-start.8 = (f32[4,128]{1,0:T(4,128)S(1)}, f32[4,128]{1,0:T(4,128)}, u32[]{:S(2)}) copy-start(f32[4,128]{1,0:T(4,128)} %param.32) | copy-start | bytes 6148
  0.7 19.0 %copy-start.7 = (s32[4,1024,32]{1,2,0:T(8,128)S(1)}, s32[4,1024,32]{1,2,0:T(8,128)}, u32[]{:S(2)}) copy-start(s32[4,1024,32]{1,2,0:T(8,128)} %param.31) | copy-start | bytes 1572868
  97.7 4.5 %copy-start.4 = (bf16[4,64,128]{2,1,0:T(8,128)(2,1)S(1)}, bf16[4,64,128]{2,1,0:T(8,128)(2,1)}, u32[]{:S(2)}) copy-start(bf16[4,64,128]{2,1,0:T(8,128)(2,1)} %param.25) | copy-start | bytes 196612
  97.7 4.5 %copy-start.5 = (bf16[4,64,128]{2,1,0:T(8,128)(2,1)S(1)}, bf16[4,64,128]{2,1,0:T(8,128)(2,1)}, u32[]{:S(2)}) copy-start(bf16[4,64,128]{2,1,0:T(8,128)(2,1)} %param.26) | copy-start | bytes 196612
  97.7 4.5 %copy-start.6 = (f32[12,64,128]{2,1,0:T(8,128)S(1)}, f32[12,64,128]{2,1,0:T(8,128)}, u32[]{:S(2)}) copy-start(f32[12,64,128]{2,1,0:T(8,128)} %get-tuple-element.12) | copy-start | bytes 1179652
  97.7 4.5 %copy-start.10 = (f32[4,128]{1,0:T(4,128)S(1)}, f32[4,128]{1,0:T(4,128)}, u32[]{:S(2)}) copy-start(f32[4,128]{1,0:T(4,128)} %param.34) | copy-start | bytes 6148
  97.7 4.5 %copy-start.11 = (f32[4,128]{1,0:T(4,128)S(1)}, f32[4,128]{1,0:T(4,128)}, u32[]{:S(2)}) copy-start(f32[4,128]{1,0:T(4,128)} %param.33) | copy-start | bytes 6148
  97.7 9.8 %copy-start.3 = (f32[4,256,128]{2,1,0:T(8,128)S(1)}, f32[4,256,128]{2,1,0:T(8,128)}, u32[]{:S(2)}) copy-start(f32[4,256,128]{2,1,0:T(8,128)} %get-tuple-element.10) | copy-start | bytes 1572868
  97.7 10.6 %copy-start.2 = (f32[4,256,128]{2,1,0:T(8,128)S(1)}, f32[4,256,128]{2,1,0:T(8,128)}, u32[]{:S(2)}) copy-start(f32[4,256,128]{2,1,0:T(8,128)} %get-tuple-element.11) | copy-start | bytes 1572868

commit v4 on v3

--- a/solution.py
+++ b/solution.py
@@ -168,41 +168,42 @@
         else:
             sum_ref[...] = both
 
-    start(z_copies[1])
+    def ready(d):
+        arrive(x_copies[d])
+        start(c_copies[1][d])
+        arrive(c_copies[0][d])
+        arrive(c_copies[1][d])
+
     start(x_copies[0])
+    for d in range(1, zs):
+        start(z_copies[d])
     start(c_copies[0][0])
     start(own)
     for copy in own:
         copy.wait()
-
-    def bring(d):
-        if d + 1 < zs:
-            left(z_copies[d])
-            start(z_copies[d + 1])
+    ready(0)
+    compute(0)
+    pc_copies[0].start()
+    for d in range(1, zs):
         arrive(z_copies[d])
         start(x_copies[d])
         start(c_copies[0][d])
-
-    for d in range(zs):
-        if 0 < d < zs - 1:
-            bring(d + 1)
-        arrive(x_copies[d])
-        start(c_copies[1][d])
-        arrive(c_copies[0][d])
-        arrive(c_copies[1][d])
+    for d in range(1, zs):
+        ready(d)
         compute(d)
         pc_copies[d].start()
-        if d == 0:
-            bring(1)
         to_x(d)
-        if d > 0:
+        if d > 1:
             to_z(d - 1)
     to_z(zs - 1)
+    to_x(0)
+    to_z(0)
     for d in range(1, zs):
         pz_copies[d].wait_recv()
         sum_ref[...] += z_in[d].astype(jnp.float32)
-    left(z_copies[zs - 1])
     for d in range(zs):
+        if d:
+            left(z_copies[d])
         left(x_copies[d])
         left(c_copies[0][d])
         left(c_copies[1][d])

time: 111 us -> 103 us (0.928)
  Pallas kernels: 76 us -> 67.5 us
    pallas_call x1, Pallas kernels: 76 us -> 67.5 us  [fused(): pl.pallas_call(functools.partial(fused_kernel, zs), out_shape=(grad, grad...]
where the time goes in v4:
time: 103 us; the launch traced here: 102 us
  Pallas kernels  67.5 us (66%)
  other arithmetic  18.4 us (18%)
  blocking collectives  10.8 us (10%)
  local copies, waits for them, and re-layouts  4.71 us (5%)
    pallas_call x1, Pallas kernels, fused(): pl.pallas_call(functools.partial(fused_kernel, zs), out_shape=(grad, grad...  67.5 us
    psum x1, blocking collectives, local(): lax.psum(jnp.concatenate([square_sums(a) for a in (vid_query, vid_key, au...  5.85 us
    psum x1, blocking collectives, local(): product = lax.psum(jnp.concatenate([p[2] for p in parts]), 'head')  4.92 us
    convert_element_type x4, other arithmetic, normalize(): (tokens.astype(jnp.float32) * scales[None, :, None] * gain_rows[:, None,...  3.53 us
    reduce_sum x3, other arithmetic, norm_parts(): return (weighted, unit_rows, jnp.sum(weighted * unit_rows, axis=(0, 2)))  2.71 us
    convert_element_type x3, other arithmetic, norm_finish(): (scales[None, :, None] * (weighted - unit_rows * mean_term[None, :, None]...  2.59 us
    reduce_sum x2, other arithmetic, square_sums(): return jnp.sum(values * values, axis=(0, 2))  2.28 us

profile of v4, /device:TPU:0, one launch (start us, length us, event | category | flops | bytes accessed | tf_op | source)
XLA Modules:
  0.0 102.2 jit_solution(2329862402136484317)
XLA Ops:
  0.6 0.0 copy-start.1
  0.7 1.1 %fusion.29 = (f32[64]{0:T(128)S(1)}, f32[64]{0:T(128)S(1)}) fusion(bf16[4,64,128]{2,1,0:T(8,128)(2,1)} %param.25, bf16[4,64,128]{2,1,0:T(8,128)(2,1)} %param.26), kind=kLoop, calls=%fused_computation.39 | loop fusion | flops 196480 | bytes 131584 | tf_op jit(solution)/shard_map/reduce_sum | solution.py:242
  1.8 1.0 multiply_reduce_fusion.1
  2.8 0.7 pad_maximum_fusion.2
  3.5 1.2 %fusion.11 = (f32[256]{0:T(256)S(1)}, f32[256]{0:T(256)S(1)}) fusion(bf16[4,256,128]{2,1,0:T(8,128)(2,1)} %param.18, bf16[4,256,128]{2,1,0:T(8,128)(2,1)} %param.19), kind=kLoop, calls=%fused_computation.15 | loop fusion | flops 785920 | bytes 526336 | tf_op jit(solution)/shard_map/reduce_sum | solution.py:242
  4.7 0.1 pad_maximum_fusion.1
  4.8 5.8 %psum.14 = f32[640]{0:T(1024)S(1)} all-reduce(f32[640]{0:T(1024)S(1)} %pad_maximum_fusion.1), channel_id=1, replica_groups=mesh['ctx'=16,'head'=2] {'head'}, use_global_device_ids=true, to_apply=%region_4.0 | all-reduce | flops 640 | bytes 5120 | tf_op jit(solution)/shard_map/psum | solution.py:266
  10.6 0.1 fusion.38
  10.7 1.2 %multiply_reduce_fusion = f32[4,256]{1,0:T(4,128)S(1)} fusion(bf16[4,256,128]{2,1,0:T(8,128)(2,1)} %param.21, bf16[4,256,128]{2,1,0:T(8,128)(2,1)} %vg_ref.1), kind=kLoop, calls=%fused_computation.22 | loop fusion | flops 523264 | bytes 528384 | tf_op jit(solution)/shard_map/reduce_sum | solution.py:271
  11.9 0.6 broadcast_in_dim.19.vd_ref
  12.5 1.3 %broadcast_in_dim.18.vl_ref = f32[4,1,256]{2,1,0:T(1,128)} reshape(f32[4,256]{1,0:T(4,128)} %param.23) | data formatting | bytes 8192 | tf_op jit(solution)/shard_map/broadcast_in_dim | solution.py:282
  13.8 0.1 tile.10
  13.9 0.6 broadcast_select_fusion.small_ref
  14.5 0.9 fusion.30
  15.5 0.9 fusion.24
  16.4 1.6 %pad_maximum_fusion.big_ref = bf16[16,64,128]{2,1,0:T(8,128)(2,1)} fusion(bf16[4,64,128]{2,1,0:T(8,128)(2,1)} %param.29, bf16[4,64,128]{2,1,0:T(8,128)(2,1)S(1)} %fusion.24, bf16[4,64,128]{2,1,0:T(8,128)(2,1)} %param.27, bf16[4,64,128]{2,1,0:T(8,128)(2,1)S(1)} %fusion.30), kind=kLoop, calls=%fused_computation.23 | loop fusion | flops 393216 | bytes 524288 | tf_op jit(solution)/shard_map/concatenate | solution.py:273
  18.0 0.8 fusion.12.vk_ref
  18.8 0.8 fusion.6.vq_ref
  19.7 2.0 %copy.24.aw_ref = s32[4,1024,32]{2,1,0:T(8,128)} copy(s32[4,1024,32]{1,2,0:T(8,128)S(1)} %copy-done.7) | data formatting | bytes 1048576 | tf_op args[13]
  21.6 67.5 %fused_grads.1 = (f32[4,256,128]{2,1,0:T(8,128)}, f32[4,256,128]{2,1,0:T(8,128)}, f32[4,256,128]{2,1,0:T(8,128)}, f32[12,64,128]{2,1,0:T(8,128)}) custom-call(bf16[16,64,128]{2,1,0:T(8,128)(2,1)} %pad_maximum_fusion.big_ref, f32[8,256]{1,0:T(8,128)} %broadcast_select_fusion.small_ref, bf16[4,256,128]{2,1,0:T(8,128)(2,1)} %fusion.6.vq_ref, ...), custom_call_target="tpu_custom_call" | custom-call | tf_op jit(solution)/shard_map/fused_grads/pallas_call | solution.py:224
  89.1 0.0 copy-start.4
  89.2 1.9 %convert_element_type.74 = bf16[4,256,128]{2,1,0:T(8,128)(2,1)} convert(f32[4,256,128]{2,1,0:T(8,128)} %get-tuple-element.13) | non-fusion elementwise | flops 131072 | bytes 786432 | tf_op jit(solution)/shard_map/convert_element_type | solution.py:297
  91.1 1.3 %fusion.7 = f32[256]{0:T(256)S(1)} fusion(bf16[4,256,128]{2,1,0:T(8,128)(2,1)S(1)} %copy-done, f32[4,256,128]{2,1,0:T(8,128)} %get-tuple-element.10, f32[4,128]{1,0:T(4,128)S(1)} %copy-done.8, f32[256]{0:T(256)S(1)} %get-tuple-element.23), kind=kLoop, calls=%fused_computation.11 | loop fusion | flops 655104 | bytes 790528 | tf_op jit(solution)/shard_map/reduce_sum | solution.py:252
  92.3 1.3 %fusion.13 = f32[256]{0:T(256)S(1)} fusion(bf16[4,256,128]{2,1,0:T(8,128)(2,1)S(1)} %copy-done.1, f32[4,256,128]{2,1,0:T(8,128)} %get-tuple-element.11, f32[4,128]{1,0:T(4,128)S(1)} %copy-done.9, f32[256]{0:T(256)S(1)} %get-tuple-element.22), kind=kLoop, calls=%fused_computation.17 | loop fusion | flops 655104 | bytes 790528 | tf_op jit(solution)/shard_map/reduce_sum | solution.py:252
  93.6 0.2 fusion.25
  93.8 0.1 pad_maximum_fusion.3
  93.9 4.9 %psum.15 = f32[640]{0:T(1024)S(1)} all-reduce(f32[640]{0:T(1024)S(1)} %pad_maximum_fusion.3), channel_id=1, replica_groups=mesh['ctx'=16,'head'=2] {'head'}, use_global_device_ids=true, to_apply=%region_11.12 | all-reduce | flops 640 | bytes 5120 | tf_op jit(solution)/shard_map/psum | solution.py:291
  98.8 0.1 slice_multiply_fusion.4
  98.9 0.9 fusion.10
  99.8 0.9 fusion.16
  100.7 0.6 slice.68
  101.4 0.8 fusion.34
  (27 shorter events, 0.1 us)
Async XLA Ops:
  0.6 17.4 %copy-start.1 = (bf16[4,256,128]{2,1,0:T(8,128)(2,1)S(1)}, bf16[4,256,128]{2,1,0:T(8,128)(2,1)}, u32[]{:S(2)}) copy-start(bf16[4,256,128]{2,1,0:T(8,128)(2,1)} %param.19) | copy-start | bytes 786436
  0.6 18.2 %copy-start = (bf16[4,256,128]{2,1,0:T(8,128)(2,1)S(1)}, bf16[4,256,128]{2,1,0:T(8,128)(2,1)}, u32[]{:S(2)}) copy-start(bf16[4,256,128]{2,1,0:T(8,128)(2,1)} %param.18) | copy-start | bytes 786436
  0.7 17.3 %copy-start.9 = (f32[4,128]{1,0:T(4,128)S(1)}, f32[4,128]{1,0:T(4,128)}, u32[]{:S(2)}) copy-start(f32[4,128]{1,0:T(4,128)} %param.35) | copy-start | bytes 6148
  0.7 18.2 %copy-start.8 = (f32[4,128]{1,0:T(4,128)S(1)}, f32[4,128]{1,0:T(4,128)}, u32[]{:S(2)}) copy-start(f32[4,128]{1,0:T(4,128)} %param.32) | copy-start | bytes 6148
  0.7 19.0 %copy-start.7 = (s32[4,1024,32]{1,2,0:T(8,128)S(1)}, s32[4,1024,32]{1,2,0:T(8,128)}, u32[]{:S(2)}) copy-start(s32[4,1024,32]{1,2,0:T(8,128)} %param.31) | copy-start | bytes 1572868
  89.1 4.5 %copy-start.4 = (bf16[4,64,128]{2,1,0:T(8,128)(2,1)S(1)}, bf16[4,64,128]{2,1,0:T(8,128)(2,1)}, u32[]{:S(2)}) copy-start(bf16[4,64,128]{2,1,0:T(8,128)(2,1)} %param.25) | copy-start | bytes 196612
  89.1 4.5 %copy-start.5 = (bf16[4,64,128]{2,1,0:T(8,128)(2,1)S(1)}, bf16[4,64,128]{2,1,0:T(8,128)(2,1)}, u32[]{:S(2)}) copy-start(bf16[4,64,128]{2,1,0:T(8,128)(2,1)} %param.26) | copy-start | bytes 196612
  89.1 4.5 %copy-start.6 = (f32[12,64,128]{2,1,0:T(8,128)S(1)}, f32[12,64,128]{2,1,0:T(8,128)}, u32[]{:S(2)}) copy-start(f32[12,64,128]{2,1,0:T(8,128)} %get-tuple-element.12) | copy-start | bytes 1179652
  89.2 4.5 %copy-start.10 = (f32[4,128]{1,0:T(4,128)S(1)}, f32[4,128]{1,0:T(4,128)}, u32[]{:S(2)}) copy-start(f32[4,128]{1,0:T(4,128)} %param.34) | copy-start | bytes 6148
  89.2 4.5 %copy-start.11 = (f32[4,128]{1,0:T(4,128)S(1)}, f32[4,128]{1,0:T(4,128)}, u32[]{:S(2)}) copy-start(f32[4,128]{1,0:T(4,128)} %param.33) | copy-start | bytes 6148
  89.2 9.8 %copy-start.3 = (f32[4,256,128]{2,1,0:T(8,128)S(1)}, f32[4,256,128]{2,1,0:T(8,128)}, u32[]{:S(2)}) copy-start(f32[4,256,128]{2,1,0:T(8,128)} %get-tuple-element.10) | copy-start | bytes 1572868
  89.2 10.6 %copy-start.2 = (f32[4,256,128]{2,1,0:T(8,128)S(1)}, f32[4,256,128]{2,1,0:T(8,128)}, u32[]{:S(2)}) copy-start(f32[4,256,128]{2,1,0:T(8,128)} %get-tuple-element.11) | copy-start | bytes 1572868

commit v5 on v4

--- a/solution.py
+++ b/solution.py
@@ -26,6 +26,8 @@
     barrier = pltpu.get_barrier_semaphore()
     targets = [peer(z, x, 1 - c), peer(z, 1 - x, c)]
     targets += [peer(lax.rem(z + d, zs), x, c) for d in range(1, zs)]
+    n, h = lax.axis_size("head"), lax.axis_index("head")
+    targets += [{"head": lax.rem(h + p, n)} for p in range(1, n)]
     for target in targets:
         pl.semaphore_signal(barrier, inc=1, device_id=target, device_id_type=MESH)
     pl.semaphore_wait(barrier, len(targets))
@@ -65,7 +67,9 @@
 
 
 def fused_kernel(zs, big_ref, small_ref, vq_ref, vk_ref, vv_ref, vg_ref, vl_ref, vd_ref, vw_ref, aw_ref,
-                 dvq_ref, dvk_ref, dvv_ref, sum_ref,
+                 vid_ref, aud_ref, vgain_ref, again_ref, vscale_ref, ascale_ref,
+                 gvq_ref, gvk_ref, gvv_ref, gaq_ref, gak_ref, gav_ref,
+                 dvq_ref, dvk_ref, dvv_ref, sum_ref, vprod, vprod_in, aprod, aprod_in, n_send, n_recv,
                  big_out, small_out, part, core_in, x_out, x_in, z_out, z_in,
                  z_send, z_recv, x_send, x_recv, c_send, c_recv, own_sem,
                  pc_send, pc_recv, px_send, px_recv, pz_send, pz_recv):
@@ -195,12 +199,53 @@
         to_x(d)
         if d > 1:
             to_z(d - 1)
+    n, me_head = vprod_in.shape[0] + 1, lax.axis_index("head")
+
+    def share(k, mine, theirs):
+        group = [pltpu.make_async_remote_copy(
+            src_ref=mine, dst_ref=theirs.at[p - 1], send_sem=n_send.at[k, p - 1], recv_sem=n_recv.at[k, p - 1],
+            device_id={"head": lax.rem(me_head + p, n)}, device_id_type=MESH) for p in range(1, n)]
+        start(group)
+        return group
+
+    def product(ups, raws, gains, scale):
+        total = sum(ups[h] * gains[h] * (raws[h].astype(jnp.float32) * scale) for h in range(heads))
+        return jnp.broadcast_to(jnp.sum(total, axis=1, keepdims=True), total.shape)
+
+    def finish(up, raw, gain, scale, total):
+        mean_term = total / (n * heads * width)
+        return (scale * (up * gain - raw.astype(jnp.float32) * scale * mean_term)).astype(jnp.bfloat16)
+
+    ups = (dvq_ref, dvk_ref)
+    for i in range(2):
+        vprod[i] = product(ups[i], vid_ref[i], vgain_ref[i], vscale_ref[i])
+    video_share = share(0, vprod, vprod_in)
+    for h in range(heads):
+        gvv_ref[h] = dvv_ref[h].astype(jnp.bfloat16)
     to_z(zs - 1)
     to_x(0)
     to_z(0)
     for d in range(1, zs):
         pz_copies[d].wait_recv()
         sum_ref[...] += z_in[d].astype(jnp.float32)
+    audio_ups = [[sum_ref[(2 - 2 * i) * heads + h] for h in range(heads)] for i in range(2)]
+    for i in range(2):
+        aprod[i] = product(audio_ups[i], aud_ref[i], again_ref[i], ascale_ref[i])
+    audio_share = share(1, aprod, aprod_in)
+    arrive(video_share)
+    for i, out in enumerate((gvq_ref, gvk_ref)):
+        total = vprod[i] + sum(vprod_in[p, i] for p in range(n - 1))
+        for h in range(heads):
+            out[h] = finish(ups[i][h], vid_ref[i, h], vgain_ref[i, h], vscale_ref[i], total)
+    for h in range(heads):
+        gav_ref[h] = sum_ref[heads + h].astype(jnp.bfloat16)
+    arrive(audio_share)
+    for i, out in enumerate((gaq_ref, gak_ref)):
+        total = aprod[i] + sum(aprod_in[p, i] for p in range(n - 1))
+        for h in range(heads):
+            out[h] = finish(audio_ups[i][h], aud_ref[i, h], again_ref[i, h], ascale_ref[i], total)
+    left(video_share)
+    left(audio_share)
     for d in range(zs):
         if d:
             left(z_copies[d])
@@ -213,20 +258,27 @@
             pz_copies[d].wait_send()
 
 
-def fused(zs, big, small, vq, vk, vv, vg, vl, vd, vw, aw):
+def fused(zs, big, small, vq, vk, vv, vg, vl, vd, vw, aw, *norms):
     rows, tokens, width = big.shape
     heads = vq.shape[0]
     lines = 3 * heads
     sems = lambda *shape: pltpu.SemaphoreType.DMA(shape)
     block = lambda *lead: pltpu.VMEM((zs, lines) + lead + (tokens, width), jnp.bfloat16)
-    grad = jax.ShapeDtypeStruct(vq.shape, jnp.float32)
+    video = vq.shape[1]
+    n = lax.axis_size("head")
+    grad = jax.ShapeDtypeStruct(vq.shape, jnp.bfloat16)
+    small_grad = jax.ShapeDtypeStruct((heads, tokens, width), jnp.bfloat16)
+    total = lambda *shape: pltpu.VMEM(shape + (width,), jnp.float32)
     vmem = pl.BlockSpec(memory_space=pltpu.VMEM)
     return pl.pallas_call(
         functools.partial(fused_kernel, zs),
-        out_shape=(grad, grad, grad, jax.ShapeDtypeStruct((lines, tokens, width), jnp.float32)),
-        in_specs=[vmem] * 10,
-        out_specs=[vmem] * 4,
+        out_shape=(grad,) * 3 + (small_grad,) * 3,
+        in_specs=[vmem] * 16,
+        out_specs=[vmem] * 6,
         scratch_shapes=[
+            total(heads, video), total(heads, video), total(heads, video), total(lines, tokens),
+            total(2, video), total(n - 1, 2, video), total(2, tokens), total(n - 1, 2, tokens),
+            sems(2, n - 1), sems(2, n - 1),
             pltpu.VMEM((rows, zs, XS, CORES, tokens, width), big.dtype),
             pltpu.VMEM((zs, XS, CORES) + small.shape, small.dtype),
             block(XS, CORES), block(XS), block(), block(), block(), block(),
@@ -234,7 +286,7 @@
         ] + [sems(zs) for _ in range(6)],
         compiler_params=pltpu.CompilerParams(collective_id=0, has_side_effects=True, vmem_limit_bytes=56 << 20),
         name="fused_grads",
-    )(big, small, vq, vk, vv, vg, vl, vd, vw, aw)
+    )(big, small, vq, vk, vv, vg, vl, vd, vw, aw, *norms)
 
 
 def square_sums(tokens):
@@ -244,17 +296,6 @@
 
 def normalize(tokens, scales, gain_rows):
     return (tokens.astype(jnp.float32) * scales[None, :, None] * gain_rows[:, None, :]).astype(jnp.bfloat16)
-
-
-def norm_parts(tokens, scales, gain_rows, upstream):
-    weighted = upstream * gain_rows[:, None, :]
-    unit_rows = tokens.astype(jnp.float32) * scales[None, :, None]
-    return (weighted, unit_rows, jnp.sum(weighted * unit_rows, axis=(0, 2)))
-
-
-def norm_finish(weighted, unit_rows, scales, product, feature_count):
-    mean_term = product / feature_count
-    return (scales[None, :, None] * (weighted - unit_rows * mean_term[None, :, None])).astype(jnp.bfloat16)
 
 
 def local(vid_query, vid_key, vid_value, vid_out, vid_grad, vid_lse, vid_mask, aud_query, aud_key, aud_value,
@@ -277,24 +318,12 @@
     small = jnp.where(
         lane_owner[None] == lax.rem(lax.axis_index("ctx"), near),
         jnp.tile(jnp.concatenate([aud_lse, audio_delta]), (1, near)), 0.0)
-    up_vq, up_vk, up_vv, sums = fused(
+    return fused(
         zs, big, small, normalize(vid_query, scale_vq, gain_vq), normalize(vid_key, scale_vk, gain_vk), vid_value,
-        vid_grad, vid_lse[:, None], video_delta[:, None], vid_mask, aud_mask)
-    sums = sums.reshape(3, heads, tokens, width)
-    up_ak, up_av, up_aq = sums[0], sums[1], sums[2]
-    parts = [
-        norm_parts(vid_query, scale_vq, gain_vq, up_vq),
-        norm_parts(vid_key, scale_vk, gain_vk, up_vk),
-        norm_parts(aud_query, scale_aq, gain_aq, up_aq),
-        norm_parts(aud_key, scale_ak, gain_ak, up_ak),
-    ]
-    product = lax.psum(jnp.concatenate([p[2] for p in parts]), "head")
-    cuts = (0, video, 2 * video, 2 * video + tokens, 2 * video + 2 * tokens)
-    done = [
-        norm_finish(w, u, scales[lo:hi], product[lo:hi], feature_count)
-        for (w, u, _), lo, hi in zip(parts, cuts[:-1], cuts[1:])
-    ]
-    return (done[0], done[1], up_vv.astype(jnp.bfloat16), done[2], done[3], up_av.astype(jnp.bfloat16))
+        vid_grad, vid_lse[:, None], video_delta[:, None], vid_mask, aud_mask,
+        jnp.stack([vid_query, vid_key]), jnp.stack([aud_query, aud_key]),
+        jnp.stack([gain_vq, gain_vk])[:, :, None], jnp.stack([gain_aq, gain_ak])[:, :, None],
+        jnp.stack([scale_vq, scale_vk])[..., None], jnp.stack([scale_aq, scale_ak])[..., None])
 
 
 def solution(mesh):

time: 103 us -> 109 us (1.058)
  local copies, waits for them, and re-layouts: 4.71 us -> 15.1 us
  blocking collectives: 10.8 us -> 5.98 us
  Pallas kernels: 67.5 us -> 71.4 us
  other arithmetic: 18.4 us -> 15.2 us
    unnamed x25 -> x21, local copies, waits for them, and re-layouts: 2.02 us -> 11.4 us
    psum x1 -> x0, blocking collectives: 4.92 us -> none  [local(): product = lax.psum(jnp.concatenate([p[2] for p in parts]), 'head')]
    convert_element_type x4 -> x0, other arithmetic: 4.48 us -> none  [the longest x3 2.59 us: norm_finish(): (scales[None, :, None] * (weighted - unit_rows * mean_term[None, :, None]...]
    another operation x0 -> x4, other arithmetic: none -> 4.08 us  [the longest x1 1.3 us: local(): jnp.stack([gain_aq, gain_ak])[:, :, None]]
    pallas_call x1, Pallas kernels: 67.5 us -> 71.4 us  [fused(): pl.pallas_call(functools.partial(fused_kernel, zs), out_shape=(grad,) * 3...]
    reduce_sum x3 -> x0, other arithmetic: 2.71 us -> none  [norm_parts(): return (weighted, unit_rows, jnp.sum(weighted * unit_rows, axis=(0, 2)))]
    broadcast_in_dim x0 -> x2, local copies, waits for them, and re-layouts: none -> 1.6 us  [the longest x1 0.86 us: local(): jnp.stack([scale_vq, scale_vk])[..., None]]
where the time goes in v5:
time: 109 us; the launch traced here: 108 us
  Pallas kernels  71.4 us (66%)
  other arithmetic  15.2 us (14%)
  local copies, waits for them, and re-layouts  15.1 us (14%)
  blocking collectives  5.98 us (5%)
    pallas_call x1, Pallas kernels, fused(): pl.pallas_call(functools.partial(fused_kernel, zs), out_shape=(grad,) * 3...  71.4 us
    unnamed x21, local copies, waits for them, and re-layouts  11.4 us
    psum x1, blocking collectives, local(): lax.psum(jnp.concatenate([square_sums(a) for a in (vid_query, vid_key, au...  5.98 us
    convert_element_type x4, other arithmetic, normalize(): (tokens.astype(jnp.float32) * scales[None, :, None] * gain_rows[:, None,...  3.53 us
    reduce_sum x2, other arithmetic, square_sums(): return jnp.sum(values * values, axis=(0, 2))  2.29 us

profile of v5, /device:TPU:0, one launch (start us, length us, event | category | flops | bytes accessed | tf_op | source)
XLA Modules:
  0.0 108.4 jit_solution(7298696396323163112)
XLA Ops:
  0.7 0.0 copy-start.1
  0.7 1.1 fusion.6
  1.8 1.0 multiply_reduce_fusion.1
  2.8 0.7 pad_maximum_fusion.4
  3.5 1.2 %fusion = (f32[256]{0:T(256)S(1)}, f32[256]{0:T(256)S(1)}) fusion(bf16[4,256,128]{2,1,0:T(8,128)(2,1)} %param.18, bf16[4,256,128]{2,1,0:T(8,128)(2,1)} %param.19), kind=kLoop, calls=%fused_computation.4 | loop fusion | flops 785920 | bytes 526336 | tf_op jit(solution)/shard_map/reduce_sum | solution.py:294
  4.7 0.1 pad_maximum_fusion.3
  4.8 6.0 %psum.7 = f32[640]{0:T(1024)S(1)} all-reduce(f32[640]{0:T(1024)S(1)} %pad_maximum_fusion.3), channel_id=1, replica_groups=mesh['ctx'=16,'head'=2] {'head'}, use_global_device_ids=true, to_apply=%region_4.0 | all-reduce | flops 640 | bytes 5120 | tf_op jit(solution)/shard_map/psum | solution.py:307
  10.8 0.1 slice_bitcast_fusion
  10.9 1.2 %multiply_reduce_fusion = f32[4,256]{1,0:T(4,128)S(1)} fusion(bf16[4,256,128]{2,1,0:T(8,128)(2,1)} %param.21, bf16[4,256,128]{2,1,0:T(8,128)(2,1)} %vg_ref.1), kind=kLoop, calls=%fused_computation.11 | loop fusion | flops 523264 | bytes 528384 | tf_op jit(solution)/shard_map/reduce_sum | solution.py:312
  12.1 0.6 broadcast_in_dim.42.vd_ref
  12.7 1.3 %broadcast_in_dim.41.vl_ref = f32[4,1,256]{2,1,0:T(1,128)} reshape(f32[4,256]{1,0:T(4,128)} %param.23) | data formatting | bytes 8192 | tf_op jit(solution)/shard_map/broadcast_in_dim | solution.py:323
  14.0 1.3 %pad_maximum_fusion.5 = f32[2,4,128]{2,1,0:T(4,128)} fusion(f32[1,4,128]{2,1,0:T(4,128)} %bitcast.30, f32[1,4,128]{2,1,0:T(4,128)} %bitcast.31), kind=kLoop, calls=%fused_computation.27 | loop fusion | flops 1024 | bytes 8192 | tf_op jit(solution)/shard_map/stack | solution.py:325
  15.3 1.3 %pad_maximum_fusion.6 = f32[2,4,128]{2,1,0:T(4,128)} fusion(f32[1,4,128]{2,1,0:T(4,128)} %bitcast.29, f32[1,4,128]{2,1,0:T(4,128)} %bitcast.28), kind=kLoop, calls=%fused_computation.28 | loop fusion | flops 1024 | bytes 8192 | tf_op jit(solution)/shard_map/stack | solution.py:325
  16.6 0.1 tile.10
  16.7 0.6 broadcast_select_fusion.small_ref
  17.3 0.7 copy.28.ascale_ref
  18.0 0.9 fusion.11
  19.0 0.9 fusion.8
  19.9 1.6 %pad_maximum_fusion.1.big_ref = bf16[16,64,128]{2,1,0:T(8,128)(2,1)} fusion(bf16[4,64,128]{2,1,0:T(8,128)(2,1)} %param.29, bf16[4,64,128]{2,1,0:T(8,128)(2,1)S(1)} %fusion.11, bf16[4,64,128]{2,1,0:T(8,128)(2,1)} %param.27, bf16[4,64,128]{2,1,0:T(8,128)(2,1)S(1)} %fusion.8), kind=kLoop, calls=%fused_computation.12 | loop fusion | flops 393216 | bytes 524288 | tf_op jit(solution)/shard_map/concatenate | solution.py:314
  21.5 0.6 pad_maximum_fusion.2.aud_ref
  22.2 0.9 copy.27.vscale_ref
  23.0 0.8 fusion.5.vk_ref
  23.9 0.8 fusion.2.vq_ref
  24.7 0.8 pad_maximum_fusion.vid_ref
  25.6 2.0 %copy.26.aw_ref = s32[4,1024,32]{2,1,0:T(8,128)} copy(s32[4,1024,32]{1,2,0:T(8,128)S(1)} %copy-done.4) | data formatting | bytes 1048576 | tf_op args[13]
  27.5 71.4 %fused_grads.1 = (bf16[4,256,128]{2,1,0:T(8,128)(2,1)}, bf16[4,256,128]{2,1,0:T(8,128)(2,1)}, bf16[4,256,128]{2,1,0:T(8,128)(2,1)}, bf16[4,64,128]{2,1,0:T(8,128...) custom-call(bf16[16,64,128]{2,1,0:T(8,128)(2,1)} %pad_maximum_fusion.1.big_ref, ...), custom_call_target="tpu_custom_call" | custom-call | tf_op jit(solution)/shard_map/fused_grads/pallas_call | solution.py:273
  99.0 1.7 %copy.35 = bf16[4,256,128]{2,1,0:T(8,128)(2,1)} copy(bf16[4,256,128]{2,1,0:T(8,128)(2,1)} %get-tuple-element.22) | data formatting | bytes 524288
  100.6 1.7 %copy.36 = bf16[4,256,128]{2,1,0:T(8,128)(2,1)} copy(bf16[4,256,128]{2,1,0:T(8,128)(2,1)} %get-tuple-element.23) | data formatting | bytes 524288
  102.3 1.7 %copy.37 = bf16[4,256,128]{2,1,0:T(8,128)(2,1)} copy(bf16[4,256,128]{2,1,0:T(8,128)(2,1)} %get-tuple-element.24) | data formatting | bytes 524288
  104.0 1.5 %copy.38 = bf16[4,64,128]{2,1,0:T(8,128)(2,1)} copy(bf16[4,64,128]{2,1,0:T(8,128)(2,1)} %get-tuple-element.25) | data formatting | bytes 131072
  105.4 1.5 %copy.39 = bf16[4,64,128]{2,1,0:T(8,128)(2,1)} copy(bf16[4,64,128]{2,1,0:T(8,128)(2,1)} %get-tuple-element.26) | data formatting | bytes 131072
  106.9 1.5 %copy.40 = bf16[4,64,128]{2,1,0:T(8,128)(2,1)} copy(bf16[4,64,128]{2,1,0:T(8,128)(2,1)} %get-tuple-element.27) | data formatting | bytes 131072
  (19 shorter events, 0.1 us)
Async XLA Ops:
  0.6 20.9 %copy-start.3 = (bf16[4,64,128]{2,1,0:T(8,128)(2,1)S(1)}, bf16[4,64,128]{2,1,0:T(8,128)(2,1)}, u32[]{:S(2)}) copy-start(bf16[4,64,128]{2,1,0:T(8,128)(2,1)} %param.26) | copy-start | bytes 196612
  0.6 20.9 %copy-start.2 = (bf16[4,64,128]{2,1,0:T(8,128)(2,1)S(1)}, bf16[4,64,128]{2,1,0:T(8,128)(2,1)}, u32[]{:S(2)}) copy-start(bf16[4,64,128]{2,1,0:T(8,128)(2,1)} %param.25) | copy-start | bytes 196612
  0.7 22.4 %copy-start.1 = (bf16[4,256,128]{2,1,0:T(8,128)(2,1)S(1)}, bf16[4,256,128]{2,1,0:T(8,128)(2,1)}, u32[]{:S(2)}) copy-start(bf16[4,256,128]{2,1,0:T(8,128)(2,1)} %param.19) | copy-start | bytes 786436
  0.7 23.2 %copy-start = (bf16[4,256,128]{2,1,0:T(8,128)(2,1)S(1)}, bf16[4,256,128]{2,1,0:T(8,128)(2,1)}, u32[]{:S(2)}) copy-start(bf16[4,256,128]{2,1,0:T(8,128)(2,1)} %param.18) | copy-start | bytes 786436
  0.7 22.4 %copy-start.5 = (f32[4,128]{1,0:T(4,128)S(1)}, f32[4,128]{1,0:T(4,128)}, u32[]{:S(2)}) copy-start(f32[4,128]{1,0:T(4,128)} %param.35) | copy-start | bytes 6148
  0.7 23.2 %copy-start.6 = (f32[4,128]{1,0:T(4,128)S(1)}, f32[4,128]{1,0:T(4,128)}, u32[]{:S(2)}) copy-start(f32[4,128]{1,0:T(4,128)} %param.32) | copy-start | bytes 6148
  4.7 20.9 %copy-start.4 = (s32[4,1024,32]{1,2,0:T(8,128)S(1)}, s32[4,1024,32]{1,2,0:T(8,128)}, u32[]{:S(2)}) copy-start(s32[4,1024,32]{1,2,0:T(8,128)} %param.31) | copy-start | bytes 1572868
